TPU v7x, 512 devices: a whole 4x4x16 slice. The times are simulated.
512 devices in a mesh: seq: 64 (over x, z), kvh: 8 (over y, core).
Axes of the slice: x: 4, y: 4, z: 16, core: 2. Of those that a mesh axis runs over, the one named last changes fastest.
Arguments:
- query_in: bfloat16 [16384, 8192], P(('seq', 'kvh')), may hold values from -8 to 8
- key_in: bfloat16 [16384, 1024], P(('seq', 'kvh')), may hold values from -8 to 8
- value_in: bfloat16 [16384, 1024], P(('seq', 'kvh')), may hold values from -6 to 6
- grad_out: bfloat16 [16384, 8192], P('seq', 'kvh'), may hold values from -6 to 6
- doc_lengths: int32 [64], replicated, may hold values from 1 to 769, 16384 in all
Outputs:
- attn_out: bfloat16 [16384, 8192], P('seq', 'kvh')
- grad_query: bfloat16 [16384, 8192], P('seq', 'kvh')
- grad_key: bfloat16 [16384, 1024], P('seq', 'kvh')
- grad_value: bfloat16 [16384, 1024], P('seq', 'kvh')
Inputs may be any that keep to these rules, and one draw needn't show every extreme that they name: `doc_lengths`: the lengths sum to 16384; the longest document has exactly 769 tokens.
All inputs are finite; a program needn't handle non-finite values.
Results may differ from a plain program's by a relative error of at most 0.03.
Values may be sent and summed in bfloat16 or wider, within the bound.
A program may use at most 64 MiB of HBM per device.

v0:
```python
import math

import jax
import jax.numpy as jnp
from jax import lax
from jax.sharding import PartitionSpec as P

HEAD_DIM = 128
SPAN = 3


def passed_along(block, axis, distance):
    devices = range(lax.axis_size(axis))
    route = [(i - distance, i) for i in devices if i - distance in devices]
    return lax.ppermute(block, axis, route)


def doc_index(positions, doc_lengths):
    doc_ends = jnp.cumsum(doc_lengths)
    return jnp.sum((doc_ends[None, :] <= positions[:, None]).astype(jnp.int32), axis=1)


def window_mask(query_pos, key_pos, doc_lengths):
    query_doc = doc_index(query_pos, doc_lengths)
    key_doc = doc_index(key_pos, doc_lengths)
    return (
        (key_pos[None, :] >= 0)
        & (key_pos[None, :] <= query_pos[:, None])
        & (key_doc[None, :] == query_doc[:, None])
    )


def head_pass(queries, key_win, value_win, grad_rows, visible, score_scale):
    scores = jnp.dot(queries, key_win.T, preferred_element_type=jnp.float32) * score_scale
    masked = jnp.where(visible, scores, -jnp.inf)
    row_max = jnp.max(masked, axis=1, keepdims=True)
    shifted_exp = jnp.exp(masked - row_max)
    prob_f32 = shifted_exp / jnp.sum(shifted_exp, axis=1, keepdims=True)
    prob_b = prob_f32.astype(jnp.bfloat16)
    attn_rows = jnp.dot(prob_b, value_win, preferred_element_type=jnp.float32).astype(jnp.bfloat16)
    row_delta = jnp.sum(
        grad_rows.astype(jnp.float32) * attn_rows.astype(jnp.float32), axis=1, keepdims=True
    )
    part_dv = jnp.dot(prob_b.T, grad_rows, preferred_element_type=jnp.float32)
    grad_prob = jnp.dot(grad_rows, value_win.T, preferred_element_type=jnp.float32)
    grad_score = (prob_f32 * (grad_prob - row_delta) * score_scale).astype(jnp.bfloat16)
    grad_rows_q = jnp.dot(grad_score, key_win, preferred_element_type=jnp.float32).astype(
        jnp.bfloat16
    )
    part_dk = jnp.dot(grad_score.T, queries, preferred_element_type=jnp.float32)
    return (attn_rows, grad_rows_q, part_dk, part_dv)


def per_device(query_in, key_in, value_in, grad_out, doc_lengths):
    query_loc, key_loc, value_loc = (
        lax.all_to_all(query_in, "kvh", split_axis=1, concat_axis=0, tiled=True),
        lax.all_to_all(key_in, "kvh", split_axis=1, concat_axis=0, tiled=True),
        lax.all_to_all(value_in, "kvh", split_axis=1, concat_axis=0, tiled=True),
    )
    tok_rows = query_loc.shape[0]
    query_heads = query_loc.shape[1] // HEAD_DIM
    pair_heads = key_loc.shape[1] // HEAD_DIM
    group_size = query_heads // pair_heads
    win_blocks = SPAN + 1
    score_scale = 1.0 / math.sqrt(HEAD_DIM)
    heads_step = max(1, min(group_size, 512 // tok_rows))
    while group_size % heads_step != 0:
        heads_step = heads_step - 1
    step_count = group_size // heads_step
    older_keys = []
    older_values = []
    for offset_back in range(SPAN, 0, -1):
        got_key, got_value = passed_along((key_loc, value_loc), "seq", offset_back)
        older_keys.append(got_key)
        older_values.append(got_value)
    key_window = jnp.concatenate(older_keys + [key_loc], axis=0)
    value_window = jnp.concatenate(older_values + [value_loc], axis=0)
    blk_idx = lax.axis_index("seq")
    query_pos = blk_idx * tok_rows + jnp.arange(tok_rows, dtype=jnp.int32)
    key_pos = (blk_idx - SPAN) * tok_rows + jnp.arange(win_blocks * tok_rows, dtype=jnp.int32)
    visible = window_mask(query_pos, key_pos, doc_lengths)
    visible_rows = jnp.tile(visible, (heads_step, 1))
    query_split = query_loc.reshape(tok_rows, pair_heads, group_size, HEAD_DIM).transpose(
        1, 2, 0, 3
    )
    query_split = query_split.reshape(pair_heads, step_count, heads_step * tok_rows, HEAD_DIM)
    grad_split = grad_out.reshape(tok_rows, pair_heads, group_size, HEAD_DIM).transpose(1, 2, 0, 3)
    grad_split = grad_split.reshape(pair_heads, step_count, heads_step * tok_rows, HEAD_DIM)
    key_split = key_window.reshape(win_blocks * tok_rows, pair_heads, HEAD_DIM).transpose(1, 0, 2)
    value_split = value_window.reshape(win_blocks * tok_rows, pair_heads, HEAD_DIM).transpose(
        1, 0, 2
    )

    def per_group(ignored, group_items):
        query_grp, grad_grp, key_one, value_one = group_items

        def per_rows(totals, row_items):
            queries, grad_rows = row_items
            attn_rows, grad_rows_q, part_dk, part_dv = head_pass(
                queries, key_one, value_one, grad_rows, visible_rows, score_scale
            )
            return ((totals[0] + part_dk, totals[1] + part_dv), (attn_rows, grad_rows_q))

        zero_acc = jnp.zeros((win_blocks * tok_rows, HEAD_DIM), jnp.float32)
        (dk_sum, dv_sum), (head_outs, head_dq) = lax.scan(
            per_rows, (zero_acc, zero_acc), (query_grp, grad_grp)
        )
        return (ignored, (head_outs, head_dq, dk_sum, dv_sum))

    ignored, (head_outs, head_dq, dk_window, dv_window) = lax.scan(
        per_group, jnp.int32(0), (query_split, grad_split, key_split, value_split)
    )
    head_outs = head_outs.reshape(pair_heads, group_size, tok_rows, HEAD_DIM)
    head_dq = head_dq.reshape(pair_heads, group_size, tok_rows, HEAD_DIM)
    attn_out = head_outs.transpose(2, 0, 1, 3).reshape(tok_rows, query_heads * HEAD_DIM)
    grad_query = head_dq.transpose(2, 0, 1, 3).reshape(tok_rows, query_heads * HEAD_DIM)
    dk_window = dk_window.transpose(1, 0, 2).reshape(win_blocks, tok_rows, pair_heads * HEAD_DIM)
    dv_window = dv_window.transpose(1, 0, 2).reshape(win_blocks, tok_rows, pair_heads * HEAD_DIM)
    grad_key = dk_window[SPAN]
    grad_value = dv_window[SPAN]
    for offset_back in range(1, SPAN + 1):
        got_dk, got_dv = passed_along(
            (dk_window[SPAN - offset_back], dv_window[SPAN - offset_back]), "seq", -offset_back
        )
        grad_key = grad_key + got_dk
        grad_value = grad_value + got_dv
    return (attn_out, grad_query, grad_key.astype(jnp.bfloat16), grad_value.astype(jnp.bfloat16))


def solution(mesh):
    placed = (
        P(("seq", "kvh"), None),
        P(("seq", "kvh"), None),
        P(("seq", "kvh"), None),
        P("seq", "kvh"),
        P(),
    )
    return jax.shard_map(
        per_device,
        mesh=mesh,
        in_specs=placed,
        out_specs=(P("seq", "kvh"), P("seq", "kvh"), P("seq", "kvh"), P("seq", "kvh")),
        check_vma=False,
    )
```

profile of v0, /device:TPU:2, one launch (start us, length us, event | category | flops | bytes accessed | tf_op | source)
XLA Modules:
  0.0 158.4 jit_solution(6352323903038156197)
XLA Ops:
  0.6 0.8 copy-done
  2.1 4.5 %all-to-all-start.1 = ((bf16[32,8,128]{2,0,1:T(8,128)(2,1)}), bf16[32,8,128]{2,0,1:T(8,128)(2,1)S(1)}, u32[]{:S(2)}, u32[]{:S(2)}) async-start(bf16[32,8,128]{2,0,1:T(8,128)(2,1)} %copy_bitcast_fusion.3), calls=%async_computation.1 | async-start | bytes 131072 | tf_op jit(solution)/shard_map/all_to_all | solution.py:57
  6.6 0.7 copy.41
  7.6 1.5 copy_bitcast_fusion.2
  9.0 1.9 %copy.61 = bf16[4,8,8,1024]{3,2,0,1:T(8,128)(2,1)} copy(bf16[4,8,8,1024]{3,2,1,0:T(8,128)(2,1)} %bitcast.121) | data formatting | bytes 1048576 | tf_op jit(solution)/shard_map/all_to_all | solution.py:56
  11.1 1.1 all-to-all-done.1
  12.2 3.7 %all-to-all-start.2 = ((bf16[32,8,128]{2,0,1:T(8,128)(2,1)}), bf16[32,8,128]{2,0,1:T(8,128)(2,1)S(1)}, u32[]{:S(2)}, u32[]{:S(2)}) async-start(bf16[32,8,128]{2,0,1:T(8,128)(2,1)} %copy_bitcast_fusion.2), calls=%async_computation.2 | async-start | bytes 131072 | tf_op jit(solution)/shard_map/all_to_all | solution.py:58
  15.9 6.5 %collective-permute-start = (bf16[256,128]{1,0:T(8,128)(2,1)S(1)}, bf16[256,128]{1,0:T(8,128)(2,1)S(1)}, u32[]{:S(2)}, u32[]{:S(2)}) collective-permute-start(bf16[256,128]{1,0:T(8,128)(2,1)S(1)} %bitcast.125), channel_id=1, source_target_pairs={{0,24},{8,32},{16,40},{24,48},{32,56},{40,64},{48,72},{56,80},{64,... | collective-permute-start | bytes 196616 | tf_op jit(solution)/shard_map/ppermute | solution.py:15
  22.5 6.4 %collective-permute-start.1 = (bf16[256,128]{1,0:T(8,128)(2,1)S(1)}, bf16[256,128]{1,0:T(8,128)(2,1)S(1)}, u32[]{:S(2)}, u32[]{:S(2)}) collective-permute-start(bf16[256,128]{1,0:T(8,128)(2,1)S(1)} %bitcast.126), channel_id=1, source_target_pairs={{0,16},{8,24},{16,32},{24,40},{32,48},{40,56},{48,64},{56,72},{64,... | collective-permute-start | bytes 196616 | tf_op jit(solution)/shard_map/ppermute | solution.py:15
  28.9 3.8 %collective-permute-start.2 = (bf16[256,128]{1,0:T(8,128)(2,1)S(1)}, bf16[256,128]{1,0:T(8,128)(2,1)S(1)}, u32[]{:S(2)}, u32[]{:S(2)}) collective-permute-start(bf16[256,128]{1,0:T(8,128)(2,1)S(1)} %bitcast.127), channel_id=1, source_target_pairs={{0,8},{8,16},{16,24},{24,32},{32,40},{40,48},{48,56},{56,64},{64,7... | collective-permute-start | bytes 196616 | tf_op jit(solution)/shard_map/ppermute | solution.py:15
  32.7 4.8 %all-to-all-start = ((bf16[32,8,1024]{2,0,1:T(8,128)(2,1)}), bf16[32,8,1024]{2,0,1:T(8,128)(2,1)S(1)}, u32[]{:S(2)}, u32[]{:S(2)}) async-start(bf16[32,8,1024]{2,0,1:T(8,128)(2,1)} %bitcast.81), calls=%async_computation | async-start | bytes 1048576 | tf_op jit(solution)/shard_map/all_to_all | solution.py:56
  38.4 6.8 %collective-permute-start.3 = (bf16[256,128]{1,0:T(8,128)(2,1)S(1)}, bf16[256,128]{1,0:T(8,128)(2,1)S(1)}, u32[]{:S(2)}, u32[]{:S(2)}) collective-permute-start(bf16[256,128]{1,0:T(8,128)(2,1)S(1)} %bitcast.129), channel_id=1, source_target_pairs={{0,24},{8,32},{16,40},{24,48},{32,56},{40,64},{48,72},{56,80},{64,... | collective-permute-start | bytes 196616 | tf_op jit(solution)/shard_map/ppermute | solution.py:15
  45.3 3.4 %collective-permute-start.4 = (bf16[256,128]{1,0:T(8,128)(2,1)S(1)}, bf16[256,128]{1,0:T(8,128)(2,1)S(1)}, u32[]{:S(2)}, u32[]{:S(2)}) collective-permute-start(bf16[256,128]{1,0:T(8,128)(2,1)S(1)} %bitcast.130), channel_id=1, source_target_pairs={{0,16},{8,24},{16,32},{24,40},{32,48},{40,56},{48,64},{56,72},{64,... | collective-permute-start | bytes 196616 | tf_op jit(solution)/shard_map/ppermute | solution.py:15
  48.7 2.9 %collective-permute-start.5 = (bf16[256,128]{1,0:T(8,128)(2,1)S(1)}, bf16[256,128]{1,0:T(8,128)(2,1)S(1)}, u32[]{:S(2)}, u32[]{:S(2)}) collective-permute-start(bf16[256,128]{1,0:T(8,128)(2,1)S(1)} %bitcast.131), channel_id=1, source_target_pairs={{0,8},{8,16},{16,24},{24,32},{32,40},{40,48},{48,56},{56,64},{64,7... | collective-permute-start | bytes 196616 | tf_op jit(solution)/shard_map/ppermute | solution.py:15
  52.4 3.5 %collective-permute-done.4 = bf16[256,128]{1,0:T(8,128)(2,1)S(1)} collective-permute-done((bf16[256,128]{1,0:T(8,128)(2,1)S(1)}, bf16[256,128]{1,0:T(8,128)(2,1)S(1)}, u32[]{:S(2)}, u32[]{:S(2)}) %collective-permute-start.4) | collective-permute-done | bytes 65568 | tf_op jit(solution)/shard_map/ppermute | solution.py:15
  55.9 1.3 collective-permute-done.5
  57.3 0.9 copy.36
  58.2 58.3 %while.30 = (s32[]{:T(128)}, f32[1024,128]{1,0:T(8,128)}, f32[1024,128]{1,0:T(8,128)}, bf16[4,512,128]{2,1,0:T(8,128)(2,1)}, bf16[4,512,128]{2,1,0:T(8,128)(2,1)...) while((s32[]{:T(128)}, f32[1024,128]{1,0:T(8,128)}, ...), condition=%wide.region_7.8_spmd.clone, body=%wide.region_3.7_spmd.clone.sunk | while | flops 815135232 | bytes 30556428 | solution.py:105
  58.2 1.9 %fusion.52 = (f32[512]{0:T(512)S(1)}, f32[512,1024]{1,0:T(8,128)S(1)}) fusion(pred[256,1024]{1,0:T(8,128)(4,1)S(1)} %get-tuple-element.309, bf16[1024,128]{1,0:T(8,128)(2,1)} %get-tuple-element.306, bf16[4,512,128]{2,1,0:T(8,128)(2,1)} %get-tuple-element.305, s32[]{:T(128)} %get-tuple-element.288), kind=kOutput, calls=%fused_computation.4.clone.1 | convolution fusion | flops 135790080 | bytes 2755072 | tf_op jit(solution)/shard_map/while/body/eval_jaxpr/while/body/eval_jaxpr/dot_general | solution.py:34
  60.1 0.7 fusion.53
  61.7 1.1 multiply_reduce_fusion.2
  62.8 1.5 multiply_convert_fusion.2
  64.3 2.2 %convolution_add_fusion.4 = f32[1024,128]{1,0:T(8,128)} fusion(bf16[512,1024]{1,0:T(8,128)(2,1)S(1)} %multiply_convert_fusion.2, f32[1024,128]{1,0:T(8,128)} %get-tuple-element.289, pred[]{:T(512)S(6)} %compare.3, bf16[4,512,128]{2,1,0:T(8,128)(2,1)} %get-tuple-element.305, s32[]{:T(128)} %get-tuple-element.288), kind=kOutput, calls=%fused_computation.8.clone.1 | convolution fusion | flops 134479872 | bytes 2228737 | tf_op jit(solution)/shard_map/while/body/eval_jaxpr/while/body/eval_jaxpr/dot_general | solution.py:50
  66.5 2.0 %fusion.55 = bf16[4,512,128]{2,1,0:T(8,128)(2,1)} fusion(bf16[4,512,128]{2,1,0:T(8,128)(2,1)} %get-tuple-element.292, s32[]{:T(128)} %get-tuple-element.288, bf16[512,1024]{1,0:T(8,128)(2,1)S(1)} %multiply_convert_fusion.2, bf16[1024,128]{1,0:T(8,128)(2,1)} %get-tuple-element.306), kind=kOutput, calls=%fused_computation.12.clone.1 | convolution fusion | flops 134283264 | bytes 1442304 | tf_op jit(solution)/shard_map/while/body/eval_jaxpr/while/body/eval_jaxpr/dot_general | solution.py:47
  68.5 1.1 copy.65
  70.3 2.2 %convolution_add_fusion.5 = f32[1024,128]{1,0:T(8,128)} fusion(f32[1024,128]{1,0:T(8,128)} %get-tuple-element.290, f32[512,1024]{1,0:T(8,128)S(1)} %fusion.54, pred[]{:T(512)S(6)} %compare.3, bf16[1,512,128]{2,1,0:T(8,128)(2,1)} %copy-done.1), kind=kOutput, calls=%fused_computation.7.clone.1 | convolution fusion | flops 135004160 | bytes 3276801 | tf_op jit(solution)/shard_map/while/body/eval_jaxpr/while/body/eval_jaxpr/dot_general | solution.py:44
  72.5 1.9 %fusion.52 = (f32[512]{0:T(512)S(1)}, f32[512,1024]{1,0:T(8,128)S(1)}) fusion(pred[256,1024]{1,0:T(8,128)(4,1)S(1)} %get-tuple-element.309, bf16[1024,128]{1,0:T(8,128)(2,1)} %get-tuple-element.306, bf16[4,512,128]{2,1,0:T(8,128)(2,1)} %get-tuple-element.305, s32[]{:T(128)} %get-tuple-element.288), kind=kOutput, calls=%fused_computation.4.clone.1 | convolution fusion | flops 135790080 | bytes 2755072 | tf_op jit(solution)/shard_map/while/body/eval_jaxpr/while/body/eval_jaxpr/dot_general | solution.py:34
  74.4 0.7 fusion.53
  75.9 1.1 multiply_reduce_fusion.2
  77.1 1.5 multiply_convert_fusion.2
  78.5 2.4 %convolution_add_fusion.4 = f32[1024,128]{1,0:T(8,128)} fusion(bf16[512,1024]{1,0:T(8,128)(2,1)S(1)} %multiply_convert_fusion.2, f32[1024,128]{1,0:T(8,128)} %get-tuple-element.289, pred[]{:T(512)S(6)} %compare.3, bf16[4,512,128]{2,1,0:T(8,128)(2,1)} %get-tuple-element.305, s32[]{:T(128)} %get-tuple-element.288), kind=kOutput, calls=%fused_computation.8.clone.1 | convolution fusion | flops 134479872 | bytes 2228737 | tf_op jit(solution)/shard_map/while/body/eval_jaxpr/while/body/eval_jaxpr/dot_general | solution.py:50
  81.0 2.0 %fusion.55 = bf16[4,512,128]{2,1,0:T(8,128)(2,1)} fusion(bf16[4,512,128]{2,1,0:T(8,128)(2,1)} %get-tuple-element.292, s32[]{:T(128)} %get-tuple-element.288, bf16[512,1024]{1,0:T(8,128)(2,1)S(1)} %multiply_convert_fusion.2, bf16[1024,128]{1,0:T(8,128)(2,1)} %get-tuple-element.306), kind=kOutput, calls=%fused_computation.12.clone.1 | convolution fusion | flops 134283264 | bytes 1442304 | tf_op jit(solution)/shard_map/while/body/eval_jaxpr/while/body/eval_jaxpr/dot_general | solution.py:47
  83.0 1.1 copy.65
  84.8 2.4 %convolution_add_fusion.5 = f32[1024,128]{1,0:T(8,128)} fusion(f32[1024,128]{1,0:T(8,128)} %get-tuple-element.290, f32[512,1024]{1,0:T(8,128)S(1)} %fusion.54, pred[]{:T(512)S(6)} %compare.3, bf16[1,512,128]{2,1,0:T(8,128)(2,1)} %copy-done.1), kind=kOutput, calls=%fused_computation.7.clone.1 | convolution fusion | flops 135004160 | bytes 3276801 | tf_op jit(solution)/shard_map/while/body/eval_jaxpr/while/body/eval_jaxpr/dot_general | solution.py:44
  87.2 1.9 %fusion.52 = (f32[512]{0:T(512)S(1)}, f32[512,1024]{1,0:T(8,128)S(1)}) fusion(pred[256,1024]{1,0:T(8,128)(4,1)S(1)} %get-tuple-element.309, bf16[1024,128]{1,0:T(8,128)(2,1)} %get-tuple-element.306, bf16[4,512,128]{2,1,0:T(8,128)(2,1)} %get-tuple-element.305, s32[]{:T(128)} %get-tuple-element.288), kind=kOutput, calls=%fused_computation.4.clone.1 | convolution fusion | flops 135790080 | bytes 2755072 | tf_op jit(solution)/shard_map/while/body/eval_jaxpr/while/body/eval_jaxpr/dot_general | solution.py:34
  89.1 0.7 fusion.53
  90.6 1.1 multiply_reduce_fusion.2
  91.8 1.5 multiply_convert_fusion.2
  93.2 2.4 %convolution_add_fusion.4 = f32[1024,128]{1,0:T(8,128)} fusion(bf16[512,1024]{1,0:T(8,128)(2,1)S(1)} %multiply_convert_fusion.2, f32[1024,128]{1,0:T(8,128)} %get-tuple-element.289, pred[]{:T(512)S(6)} %compare.3, bf16[4,512,128]{2,1,0:T(8,128)(2,1)} %get-tuple-element.305, s32[]{:T(128)} %get-tuple-element.288), kind=kOutput, calls=%fused_computation.8.clone.1 | convolution fusion | flops 134479872 | bytes 2228737 | tf_op jit(solution)/shard_map/while/body/eval_jaxpr/while/body/eval_jaxpr/dot_general | solution.py:50
  95.7 2.0 %fusion.55 = bf16[4,512,128]{2,1,0:T(8,128)(2,1)} fusion(bf16[4,512,128]{2,1,0:T(8,128)(2,1)} %get-tuple-element.292, s32[]{:T(128)} %get-tuple-element.288, bf16[512,1024]{1,0:T(8,128)(2,1)S(1)} %multiply_convert_fusion.2, bf16[1024,128]{1,0:T(8,128)(2,1)} %get-tuple-element.306), kind=kOutput, calls=%fused_computation.12.clone.1 | convolution fusion | flops 134283264 | bytes 1442304 | tf_op jit(solution)/shard_map/while/body/eval_jaxpr/while/body/eval_jaxpr/dot_general | solution.py:47
  97.7 1.1 copy.65
  99.5 2.4 %convolution_add_fusion.5 = f32[1024,128]{1,0:T(8,128)} fusion(f32[1024,128]{1,0:T(8,128)} %get-tuple-element.290, f32[512,1024]{1,0:T(8,128)S(1)} %fusion.54, pred[]{:T(512)S(6)} %compare.3, bf16[1,512,128]{2,1,0:T(8,128)(2,1)} %copy-done.1), kind=kOutput, calls=%fused_computation.7.clone.1 | convolution fusion | flops 135004160 | bytes 3276801 | tf_op jit(solution)/shard_map/while/body/eval_jaxpr/while/body/eval_jaxpr/dot_general | solution.py:44
  101.9 1.9 %fusion.52 = (f32[512]{0:T(512)S(1)}, f32[512,1024]{1,0:T(8,128)S(1)}) fusion(pred[256,1024]{1,0:T(8,128)(4,1)S(1)} %get-tuple-element.309, bf16[1024,128]{1,0:T(8,128)(2,1)} %get-tuple-element.306, bf16[4,512,128]{2,1,0:T(8,128)(2,1)} %get-tuple-element.305, s32[]{:T(128)} %get-tuple-element.288), kind=kOutput, calls=%fused_computation.4.clone.1 | convolution fusion | flops 135790080 | bytes 2755072 | tf_op jit(solution)/shard_map/while/body/eval_jaxpr/while/body/eval_jaxpr/dot_general | solution.py:34
  105.3 1.1 multiply_reduce_fusion.2
  106.5 1.5 multiply_convert_fusion.2
  107.9 2.4 %convolution_add_fusion.4 = f32[1024,128]{1,0:T(8,128)} fusion(bf16[512,1024]{1,0:T(8,128)(2,1)S(1)} %multiply_convert_fusion.2, f32[1024,128]{1,0:T(8,128)} %get-tuple-element.289, pred[]{:T(512)S(6)} %compare.3, bf16[4,512,128]{2,1,0:T(8,128)(2,1)} %get-tuple-element.305, s32[]{:T(128)} %get-tuple-element.288), kind=kOutput, calls=%fused_computation.8.clone.1 | convolution fusion | flops 134479872 | bytes 2228737 | tf_op jit(solution)/shard_map/while/body/eval_jaxpr/while/body/eval_jaxpr/dot_general | solution.py:50
  110.4 2.0 %fusion.55 = bf16[4,512,128]{2,1,0:T(8,128)(2,1)} fusion(bf16[4,512,128]{2,1,0:T(8,128)(2,1)} %get-tuple-element.292, s32[]{:T(128)} %get-tuple-element.288, bf16[512,1024]{1,0:T(8,128)(2,1)S(1)} %multiply_convert_fusion.2, bf16[1024,128]{1,0:T(8,128)(2,1)} %get-tuple-element.306), kind=kOutput, calls=%fused_computation.12.clone.1 | convolution fusion | flops 134283264 | bytes 1442304 | tf_op jit(solution)/shard_map/while/body/eval_jaxpr/while/body/eval_jaxpr/dot_general | solution.py:47
  112.4 1.1 copy.65
  114.2 2.4 %convolution_add_fusion.5 = f32[1024,128]{1,0:T(8,128)} fusion(f32[1024,128]{1,0:T(8,128)} %get-tuple-element.290, f32[512,1024]{1,0:T(8,128)S(1)} %fusion.54, pred[]{:T(512)S(6)} %compare.3, bf16[1,512,128]{2,1,0:T(8,128)(2,1)} %copy-done.1), kind=kOutput, calls=%fused_computation.7.clone.1 | convolution fusion | flops 135004160 | bytes 3276801 | tf_op jit(solution)/shard_map/while/body/eval_jaxpr/while/body/eval_jaxpr/dot_general | solution.py:44
  116.6 1.1 fusion.18
  117.7 3.1 %collective-permute-start.10 = (f32[256,128]{1,0:T(8,128)S(1)}, f32[256,128]{1,0:T(8,128)S(1)}, u32[]{:S(2)}, u32[]{:S(2)}) collective-permute-start(f32[256,128]{1,0:T(8,128)S(1)} %get-tuple-element.203), channel_id=1, source_target_pairs={{16,0},{24,8},{32,16},{40,24},{48,32},{56,40},{64,48},{72,56},{80,... | collective-permute-start | bytes 393224 | tf_op jit(solution)/shard_map/ppermute | solution.py:15
  120.8 2.4 %collective-permute-start.11 = (f32[256,128]{1,0:T(8,128)S(1)}, f32[256,128]{1,0:T(8,128)S(1)}, u32[]{:S(2)}, u32[]{:S(2)}) collective-permute-start(f32[256,128]{1,0:T(8,128)S(1)} %get-tuple-element.202), channel_id=1, source_target_pairs={{24,0},{32,8},{40,16},{48,24},{56,32},{64,40},{72,48},{80,56},{88,... | collective-permute-start | bytes 393224 | tf_op jit(solution)/shard_map/ppermute | solution.py:15
  123.2 2.5 %collective-permute-start.9 = (f32[256,128]{1,0:T(8,128)S(1)}, f32[256,128]{1,0:T(8,128)S(1)}, u32[]{:S(2)}, u32[]{:S(2)}) collective-permute-start(f32[256,128]{1,0:T(8,128)S(1)} %get-tuple-element.201), channel_id=1, source_target_pairs={{8,0},{16,8},{24,16},{32,24},{40,32},{48,40},{56,48},{64,56},{72,6... | collective-permute-start | bytes 393224 | tf_op jit(solution)/shard_map/ppermute | solution.py:15
  125.7 1.1 fusion.19
  126.7 2.7 %collective-permute-start.6 = (f32[256,128]{1,0:T(8,128)S(1)}, f32[256,128]{1,0:T(8,128)S(1)}, u32[]{:S(2)}, u32[]{:S(2)}) collective-permute-start(f32[256,128]{1,0:T(8,128)S(1)} %get-tuple-element.204), channel_id=1, source_target_pairs={{8,0},{16,8},{24,16},{32,24},{40,32},{48,40},{56,48},{64,56},{72,6... | collective-permute-start | bytes 393224 | tf_op jit(solution)/shard_map/ppermute | solution.py:15
  129.5 5.5 %collective-permute-start.7 = (f32[256,128]{1,0:T(8,128)S(1)}, f32[256,128]{1,0:T(8,128)S(1)}, u32[]{:S(2)}, u32[]{:S(2)}) collective-permute-start(f32[256,128]{1,0:T(8,128)S(1)} %get-tuple-element.206), channel_id=1, source_target_pairs={{16,0},{24,8},{32,16},{40,24},{48,32},{56,40},{64,48},{72,56},{80,... | collective-permute-start | bytes 393224 | tf_op jit(solution)/shard_map/ppermute | solution.py:15
  135.0 1.4 copy.46
  136.4 0.9 copy.60
  137.5 1.0 copy.47
  138.5 5.5 %collective-permute-start.8 = (f32[256,128]{1,0:T(8,128)S(1)}, f32[256,128]{1,0:T(8,128)S(1)}, u32[]{:S(2)}, u32[]{:S(2)}) collective-permute-start(f32[256,128]{1,0:T(8,128)S(1)} %get-tuple-element.205), channel_id=1, source_target_pairs={{24,0},{32,8},{40,16},{48,24},{56,32},{64,40},{72,48},{80,56},{88,... | collective-permute-start | bytes 393224 | tf_op jit(solution)/shard_map/ppermute | solution.py:15
  144.0 1.6 add_convert_fusion
  145.6 3.9 %collective-permute-done.7 = f32[256,128]{1,0:T(8,128)S(1)} collective-permute-done((f32[256,128]{1,0:T(8,128)S(1)}, f32[256,128]{1,0:T(8,128)S(1)}, u32[]{:S(2)}, u32[]{:S(2)}) %collective-permute-start.7) | collective-permute-done | bytes 131104 | tf_op jit(solution)/shard_map/ppermute | solution.py:15
  149.5 7.4 %collective-permute-done.8 = f32[256,128]{1,0:T(8,128)S(1)} collective-permute-done((f32[256,128]{1,0:T(8,128)S(1)}, f32[256,128]{1,0:T(8,128)S(1)}, u32[]{:S(2)}, u32[]{:S(2)}) %collective-permute-start.8) | collective-permute-done | bytes 131104 | tf_op jit(solution)/shard_map/ppermute | solution.py:15
  156.9 1.6 add_convert_fusion.1
  (91 shorter events, 9.4 us)
Async XLA Ops:
  0.6 0.8 copy-start
  1.5 36.5 %copy-start.6 = (bf16[256,1024]{1,0:T(8,128)(2,1)S(1)}, bf16[256,1024]{1,0:T(8,128)(2,1)}, u32[]{:S(2)}) copy-start(bf16[256,1024]{1,0:T(8,128)(2,1)} %param.10) | copy-start | bytes 1572868
  2.1 10.1 %all-to-all-start.1 = ((bf16[32,8,128]{2,0,1:T(8,128)(2,1)}), bf16[32,8,128]{2,0,1:T(8,128)(2,1)S(1)}, u32[]{:S(2)}, u32[]{:S(2)}) async-start(bf16[32,8,128]{2,0,1:T(8,128)(2,1)} %copy_bitcast_fusion.3), calls=%async_computation.1 | async-start | bytes 131072 | tf_op jit(solution)/shard_map/all_to_all | solution.py:57
  12.2 20.5 %all-to-all-start.2 = ((bf16[32,8,128]{2,0,1:T(8,128)(2,1)}), bf16[32,8,128]{2,0,1:T(8,128)(2,1)S(1)}, u32[]{:S(2)}, u32[]{:S(2)}) async-start(bf16[32,8,128]{2,0,1:T(8,128)(2,1)} %copy_bitcast_fusion.2), calls=%async_computation.2 | async-start | bytes 131072 | tf_op jit(solution)/shard_map/all_to_all | solution.py:58
  15.9 32.7 %collective-permute-start = (bf16[256,128]{1,0:T(8,128)(2,1)S(1)}, bf16[256,128]{1,0:T(8,128)(2,1)S(1)}, u32[]{:S(2)}, u32[]{:S(2)}) collective-permute-start(bf16[256,128]{1,0:T(8,128)(2,1)S(1)} %bitcast.125), channel_id=1, source_target_pairs={{0,24},{8,32},{16,40},{24,48},{32,56},{40,64},{48,72},{56,80},{64,... | collective-permute-start | bytes 196616 | tf_op jit(solution)/shard_map/ppermute | solution.py:15
  22.5 29.1 %collective-permute-start.1 = (bf16[256,128]{1,0:T(8,128)(2,1)S(1)}, bf16[256,128]{1,0:T(8,128)(2,1)S(1)}, u32[]{:S(2)}, u32[]{:S(2)}) collective-permute-start(bf16[256,128]{1,0:T(8,128)(2,1)S(1)} %bitcast.126), channel_id=1, source_target_pairs={{0,16},{8,24},{16,32},{24,40},{32,48},{40,56},{48,64},{56,72},{64,... | collective-permute-start | bytes 196616 | tf_op jit(solution)/shard_map/ppermute | solution.py:15
  28.9 22.7 %collective-permute-start.2 = (bf16[256,128]{1,0:T(8,128)(2,1)S(1)}, bf16[256,128]{1,0:T(8,128)(2,1)S(1)}, u32[]{:S(2)}, u32[]{:S(2)}) collective-permute-start(bf16[256,128]{1,0:T(8,128)(2,1)S(1)} %bitcast.127), channel_id=1, source_target_pairs={{0,8},{8,16},{16,24},{24,32},{32,40},{40,48},{48,56},{56,64},{64,7... | collective-permute-start | bytes 196616 | tf_op jit(solution)/shard_map/ppermute | solution.py:15
  32.7 24.5 %all-to-all-start = ((bf16[32,8,1024]{2,0,1:T(8,128)(2,1)}), bf16[32,8,1024]{2,0,1:T(8,128)(2,1)S(1)}, u32[]{:S(2)}, u32[]{:S(2)}) async-start(bf16[32,8,1024]{2,0,1:T(8,128)(2,1)} %bitcast.81), calls=%async_computation | async-start | bytes 1048576 | tf_op jit(solution)/shard_map/all_to_all | solution.py:56
  38.4 13.9 %collective-permute-start.3 = (bf16[256,128]{1,0:T(8,128)(2,1)S(1)}, bf16[256,128]{1,0:T(8,128)(2,1)S(1)}, u32[]{:S(2)}, u32[]{:S(2)}) collective-permute-start(bf16[256,128]{1,0:T(8,128)(2,1)S(1)} %bitcast.129), channel_id=1, source_target_pairs={{0,24},{8,32},{16,40},{24,48},{32,56},{40,64},{48,72},{56,80},{64,... | collective-permute-start | bytes 196616 | tf_op jit(solution)/shard_map/ppermute | solution.py:15
  45.3 10.6 %collective-permute-start.4 = (bf16[256,128]{1,0:T(8,128)(2,1)S(1)}, bf16[256,128]{1,0:T(8,128)(2,1)S(1)}, u32[]{:S(2)}, u32[]{:S(2)}) collective-permute-start(bf16[256,128]{1,0:T(8,128)(2,1)S(1)} %bitcast.130), channel_id=1, source_target_pairs={{0,16},{8,24},{16,32},{24,40},{32,48},{40,56},{48,64},{56,72},{64,... | collective-permute-start | bytes 196616 | tf_op jit(solution)/shard_map/ppermute | solution.py:15
  48.7 8.5 %collective-permute-start.5 = (bf16[256,128]{1,0:T(8,128)(2,1)S(1)}, bf16[256,128]{1,0:T(8,128)(2,1)S(1)}, u32[]{:S(2)}, u32[]{:S(2)}) collective-permute-start(bf16[256,128]{1,0:T(8,128)(2,1)S(1)} %bitcast.131), channel_id=1, source_target_pairs={{0,8},{8,16},{16,24},{24,32},{32,40},{40,48},{48,56},{56,64},{64,7... | collective-permute-start | bytes 196616 | tf_op jit(solution)/shard_map/ppermute | solution.py:15
  58.2 3.3 %copy-start.4 = (bf16[4,512,128]{2,1,0:T(8,128)(2,1)}, bf16[4,512,128]{2,1,0:T(8,128)(2,1)S(1)}, u32[]{:S(2)}) copy-start(bf16[4,512,128]{2,1,0:T(8,128)(2,1)S(1)} %get-tuple-element.307) | copy-start | bytes 1572868 | tf_op jit(solution)/shard_map/while/body/eval_jaxpr/while
  58.2 3.4 %copy-start.2 = (bf16[1024,128]{1,0:T(8,128)(2,1)}, bf16[1024,128]{1,0:T(8,128)(2,1)S(1)}, u32[]{:S(2)}) copy-start(bf16[1024,128]{1,0:T(8,128)(2,1)S(1)} %get-tuple-element.308) | copy-start | bytes 786436 | tf_op jit(solution)/shard_map/while/body/eval_jaxpr/while
  61.5 1.3 copy-start.1
  68.5 4.0 %copy-start.3 = (bf16[1024,128]{1,0:T(8,128)(2,1)S(1)}, bf16[1024,128]{1,0:T(8,128)(2,1)}, u32[]{:S(2)}) copy-start(bf16[1024,128]{1,0:T(8,128)(2,1)} %copy-done.2) | copy-start | bytes 786436 | tf_op jit(solution)/shard_map/while/body/eval_jaxpr/while
  68.5 4.0 %copy-start.5 = (bf16[4,512,128]{2,1,0:T(8,128)(2,1)S(1)}, bf16[4,512,128]{2,1,0:T(8,128)(2,1)}, u32[]{:S(2)}) copy-start(bf16[4,512,128]{2,1,0:T(8,128)(2,1)} %copy-done.4) | copy-start | bytes 1572868 | tf_op jit(solution)/shard_map/while/body/eval_jaxpr/while
  72.5 3.3 %copy-start.4 = (bf16[4,512,128]{2,1,0:T(8,128)(2,1)}, bf16[4,512,128]{2,1,0:T(8,128)(2,1)S(1)}, u32[]{:S(2)}) copy-start(bf16[4,512,128]{2,1,0:T(8,128)(2,1)S(1)} %get-tuple-element.307) | copy-start | bytes 1572868 | tf_op jit(solution)/shard_map/while/body/eval_jaxpr/while
  72.5 3.4 %copy-start.2 = (bf16[1024,128]{1,0:T(8,128)(2,1)}, bf16[1024,128]{1,0:T(8,128)(2,1)S(1)}, u32[]{:S(2)}) copy-start(bf16[1024,128]{1,0:T(8,128)(2,1)S(1)} %get-tuple-element.308) | copy-start | bytes 786436 | tf_op jit(solution)/shard_map/while/body/eval_jaxpr/while
  75.8 1.3 copy-start.1
  83.0 4.2 %copy-start.3 = (bf16[1024,128]{1,0:T(8,128)(2,1)S(1)}, bf16[1024,128]{1,0:T(8,128)(2,1)}, u32[]{:S(2)}) copy-start(bf16[1024,128]{1,0:T(8,128)(2,1)} %copy-done.2) | copy-start | bytes 786436 | tf_op jit(solution)/shard_map/while/body/eval_jaxpr/while
  83.0 4.2 %copy-start.5 = (bf16[4,512,128]{2,1,0:T(8,128)(2,1)S(1)}, bf16[4,512,128]{2,1,0:T(8,128)(2,1)}, u32[]{:S(2)}) copy-start(bf16[4,512,128]{2,1,0:T(8,128)(2,1)} %copy-done.4) | copy-start | bytes 1572868 | tf_op jit(solution)/shard_map/while/body/eval_jaxpr/while
  87.2 3.3 %copy-start.4 = (bf16[4,512,128]{2,1,0:T(8,128)(2,1)}, bf16[4,512,128]{2,1,0:T(8,128)(2,1)S(1)}, u32[]{:S(2)}) copy-start(bf16[4,512,128]{2,1,0:T(8,128)(2,1)S(1)} %get-tuple-element.307) | copy-start | bytes 1572868 | tf_op jit(solution)/shard_map/while/body/eval_jaxpr/while
  87.2 3.4 %copy-start.2 = (bf16[1024,128]{1,0:T(8,128)(2,1)}, bf16[1024,128]{1,0:T(8,128)(2,1)S(1)}, u32[]{:S(2)}) copy-start(bf16[1024,128]{1,0:T(8,128)(2,1)S(1)} %get-tuple-element.308) | copy-start | bytes 786436 | tf_op jit(solution)/shard_map/while/body/eval_jaxpr/while
  90.5 1.3 copy-start.1
  97.7 4.2 %copy-start.3 = (bf16[1024,128]{1,0:T(8,128)(2,1)S(1)}, bf16[1024,128]{1,0:T(8,128)(2,1)}, u32[]{:S(2)}) copy-start(bf16[1024,128]{1,0:T(8,128)(2,1)} %copy-done.2) | copy-start | bytes 786436 | tf_op jit(solution)/shard_map/while/body/eval_jaxpr/while
  97.7 4.2 %copy-start.5 = (bf16[4,512,128]{2,1,0:T(8,128)(2,1)S(1)}, bf16[4,512,128]{2,1,0:T(8,128)(2,1)}, u32[]{:S(2)}) copy-start(bf16[4,512,128]{2,1,0:T(8,128)(2,1)} %copy-done.4) | copy-start | bytes 1572868 | tf_op jit(solution)/shard_map/while/body/eval_jaxpr/while
  101.9 3.3 %copy-start.4 = (bf16[4,512,128]{2,1,0:T(8,128)(2,1)}, bf16[4,512,128]{2,1,0:T(8,128)(2,1)S(1)}, u32[]{:S(2)}) copy-start(bf16[4,512,128]{2,1,0:T(8,128)(2,1)S(1)} %get-tuple-element.307) | copy-start | bytes 1572868 | tf_op jit(solution)/shard_map/while/body/eval_jaxpr/while
  101.9 3.4 %copy-start.2 = (bf16[1024,128]{1,0:T(8,128)(2,1)}, bf16[1024,128]{1,0:T(8,128)(2,1)S(1)}, u32[]{:S(2)}) copy-start(bf16[1024,128]{1,0:T(8,128)(2,1)S(1)} %get-tuple-element.308) | copy-start | bytes 786436 | tf_op jit(solution)/shard_map/while/body/eval_jaxpr/while
  105.2 1.3 copy-start.1
  112.4 4.2 %copy-start.3 = (bf16[1024,128]{1,0:T(8,128)(2,1)S(1)}, bf16[1024,128]{1,0:T(8,128)(2,1)}, u32[]{:S(2)}) copy-start(bf16[1024,128]{1,0:T(8,128)(2,1)} %copy-done.2) | copy-start | bytes 786436 | tf_op jit(solution)/shard_map/while/body/eval_jaxpr/while
  112.4 4.2 %copy-start.5 = (bf16[4,512,128]{2,1,0:T(8,128)(2,1)S(1)}, bf16[4,512,128]{2,1,0:T(8,128)(2,1)}, u32[]{:S(2)}) copy-start(bf16[4,512,128]{2,1,0:T(8,128)(2,1)} %copy-done.4) | copy-start | bytes 1572868 | tf_op jit(solution)/shard_map/while/body/eval_jaxpr/while
  116.6 20.7 %copy-start.7 = (bf16[4,512,128]{2,1,0:T(8,128)(2,1)S(1)}, bf16[4,512,128]{2,1,0:T(8,128)(2,1)}, u32[]{:S(2)}) copy-start(bf16[4,512,128]{2,1,0:T(8,128)(2,1)} %get-tuple-element.89) | copy-start | bytes 1572868
  117.7 20.8 %collective-permute-start.10 = (f32[256,128]{1,0:T(8,128)S(1)}, f32[256,128]{1,0:T(8,128)S(1)}, u32[]{:S(2)}, u32[]{:S(2)}) collective-permute-start(f32[256,128]{1,0:T(8,128)S(1)} %get-tuple-element.203), channel_id=1, source_target_pairs={{16,0},{24,8},{32,16},{40,24},{48,32},{56,40},{64,48},{72,56},{80,... | collective-permute-start | bytes 393224 | tf_op jit(solution)/shard_map/ppermute | solution.py:15
  120.8 23.2 %collective-permute-start.11 = (f32[256,128]{1,0:T(8,128)S(1)}, f32[256,128]{1,0:T(8,128)S(1)}, u32[]{:S(2)}, u32[]{:S(2)}) collective-permute-start(f32[256,128]{1,0:T(8,128)S(1)} %get-tuple-element.202), channel_id=1, source_target_pairs={{24,0},{32,8},{40,16},{48,24},{56,32},{64,40},{72,48},{80,56},{88,... | collective-permute-start | bytes 393224 | tf_op jit(solution)/shard_map/ppermute | solution.py:15
  123.2 20.8 %collective-permute-start.9 = (f32[256,128]{1,0:T(8,128)S(1)}, f32[256,128]{1,0:T(8,128)S(1)}, u32[]{:S(2)}, u32[]{:S(2)}) collective-permute-start(f32[256,128]{1,0:T(8,128)S(1)} %get-tuple-element.201), channel_id=1, source_target_pairs={{8,0},{16,8},{24,16},{32,24},{40,32},{48,40},{56,48},{64,56},{72,6... | collective-permute-start | bytes 393224 | tf_op jit(solution)/shard_map/ppermute | solution.py:15
  126.7 18.9 %collective-permute-start.6 = (f32[256,128]{1,0:T(8,128)S(1)}, f32[256,128]{1,0:T(8,128)S(1)}, u32[]{:S(2)}, u32[]{:S(2)}) collective-permute-start(f32[256,128]{1,0:T(8,128)S(1)} %get-tuple-element.204), channel_id=1, source_target_pairs={{8,0},{16,8},{24,16},{32,24},{40,32},{48,40},{56,48},{64,56},{72,6... | collective-permute-start | bytes 393224 | tf_op jit(solution)/shard_map/ppermute | solution.py:15
  129.5 20.0 %collective-permute-start.7 = (f32[256,128]{1,0:T(8,128)S(1)}, f32[256,128]{1,0:T(8,128)S(1)}, u32[]{:S(2)}, u32[]{:S(2)}) collective-permute-start(f32[256,128]{1,0:T(8,128)S(1)} %get-tuple-element.206), channel_id=1, source_target_pairs={{16,0},{24,8},{32,16},{40,24},{48,32},{56,40},{64,48},{72,56},{80,... | collective-permute-start | bytes 393224 | tf_op jit(solution)/shard_map/ppermute | solution.py:15
  138.5 18.4 %collective-permute-start.8 = (f32[256,128]{1,0:T(8,128)S(1)}, f32[256,128]{1,0:T(8,128)S(1)}, u32[]{:S(2)}, u32[]{:S(2)}) collective-permute-start(f32[256,128]{1,0:T(8,128)S(1)} %get-tuple-element.205), channel_id=1, source_target_pairs={{24,0},{32,8},{40,16},{48,24},{56,32},{64,40},{72,48},{80,56},{88,... | collective-permute-start | bytes 393224 | tf_op jit(solution)/shard_map/ppermute | solution.py:15
where the time goes:
time: 160 us; the launch traced here: 158 us
  starting transfers between devices  64.6 us (40%)
  matrix products  45 us (28%)
  local copies, waits for them, and re-layouts  20.4 us (13%)
  waiting for transfers between devices  17.3 us (11%)
  other arithmetic  9.99 us (6%)
    ppermute x12, starting transfers between devices, passed_along(): return lax.ppermute(block, axis, route)  51.6 us
    ppermute x12, waiting for transfers between devices, passed_along(): return lax.ppermute(block, axis, route)  16.2 us
    dot_general x4, matrix products, head_pass(): part_dk = jnp.dot(grad_score.T, queries, preferred_element_type=jnp.float32)  9.51 us
    dot_general x4, matrix products, head_pass(): part_dv = jnp.dot(prob_b.T, grad_rows, preferred_element_type=jnp.float32)  9.33 us
    dot_general x4, matrix products, head_pass(): jnp.dot(grad_score, key_win, preferred_element_type=jnp.float32)  8.17 us
    dot_general x4, matrix products, head_pass(): jnp.dot(queries, key_win.T, preferred_element_type=jnp.float32)  7.61 us
    dynamic_update_slice x8, local copies, waits for them, and re-layouts, per_group(): lax.scan(per_rows, (zero_acc, zero_acc), (query_grp, grad_grp))  7.05 us
    dot_general x4, matrix products, head_pass(): jnp.dot(grad_rows, value_win.T, preferred_element_type=jnp.float32)  5.84 us
  transfers between devices with their start and end apart: 15, of which 5 were waited for; matrix products, arithmetic and copies ran while one was open for 8% of the time, Pallas kernels for 0%

commit v1 on v0

v1 whole, which is shorter than its diff:
```python
import functools
import math

import jax
import jax.numpy as jnp
from jax import lax
from jax.experimental import pallas as pl
from jax.experimental.pallas import tpu as pltpu
from jax.sharding import PartitionSpec as P

MESH = pl.DeviceIdType.MESH
D = 128
SPAN = 3
WIN = SPAN + 1
ONES = 16
HIDDEN = -1e30
SCALE = 1.0 / math.sqrt(D)
SCALE_2 = SCALE * math.log2(math.e)
PAIR = 2


def dot(a, b):
    return jnp.dot(a, b, preferred_element_type=jnp.float32)


def dot_nt(a, b):
    return lax.dot_general(a, b, (((1,), (1,)), ((), ())), preferred_element_type=jnp.float32)


def kernel(
    n_seq,
    n_kvh,
    doc_ref,
    q_hbm,
    k_hbm,
    v_hbm,
    do_hbm,
    attn_ref,
    dq_ref,
    dk_ref,
    dv_ref,
    q_loc,
    do_loc,
    q_s,
    do_s,
    do_t,
    kv,
    k_t,
    v_t,
    bias,
    prob_s,
    max_s,
    out_t,
    attn_t,
    dq_t,
    ratio_s,
    delta_s,
    part,
    snd,
    rcv,
    local_sem,
    a2a_send,
    a2a_recv,
    halo_send,
    halo_recv,
    back_send,
    back_recv,
):
    rows, cols = do_loc.shape
    chunks, wide = q_s.shape[0], q_s.shape[1]
    pair = wide // rows
    per_half = chunks // 2
    piece = q_hbm.shape[0]
    s, g = lax.axis_index("seq"), lax.axis_index("kvh")
    nxt, prv = lax.rem(s + 1, n_seq), lax.rem(s + n_seq - 1, n_seq)

    def columns(h, width=D):
        return pl.ds(pl.multiple_of(h * width, width), width)

    mine = pl.ds(pl.multiple_of(g * piece, piece), piece)

    locals_ = [
        pltpu.make_async_copy(k_hbm.at[:, columns(g)], kv.at[SPAN, 0, mine, :], local_sem.at[0]),
        pltpu.make_async_copy(v_hbm.at[:, columns(g)], kv.at[SPAN, 1, mine, :], local_sem.at[1]),
        pltpu.make_async_copy(do_hbm, do_loc, local_sem.at[2]),
        pltpu.make_async_copy(q_hbm.at[:, columns(g, cols)], q_loc.at[mine, :], local_sem.at[3]),
    ]
    for copy in locals_:
        copy.start()

    barrier = pltpu.get_barrier_semaphore()
    for j in range(1, n_kvh):
        pl.semaphore_signal(
            barrier, inc=1, device_id=(s, lax.rem(g + j, n_kvh)), device_id_type=MESH
        )
    for to in (nxt, prv):
        pl.semaphore_signal(barrier, inc=1, device_id=(to, g), device_id_type=MESH)
    pl.semaphore_wait(barrier, n_kvh + 1)

    def to_peer(kind, j):
        peer = lax.rem(g + j, n_kvh)
        if kind >= 2:
            half = cols // 2
            src = q_hbm.at[:, columns(2 * peer + kind - 2, half)]
            dst = q_loc.at[mine, pl.ds((kind - 2) * half, half)]
        else:
            src = (k_hbm, v_hbm)[kind].at[:, columns(peer)]
            dst = kv.at[SPAN, kind, mine, :]
        return pltpu.make_async_remote_copy(
            src_ref=src,
            dst_ref=dst,
            send_sem=a2a_send.at[kind, j - 1],
            recv_sem=a2a_recv.at[kind, j - 1],
            device_id=(s, peer),
            device_id_type=MESH,
        )

    sends = [[to_peer(kind, j) for j in range(1, n_kvh)] for kind in range(4)]
    for kind in range(4):
        for copy in sends[kind]:
            copy.start()

    def halo(hop, kind):
        return pltpu.make_async_remote_copy(
            src_ref=kv.at[SPAN - hop, kind],
            dst_ref=kv.at[SPAN - hop - 1, kind],
            send_sem=halo_send.at[hop, kind],
            recv_sem=halo_recv.at[hop, kind],
            device_id=(nxt, g),
            device_id_type=MESH,
        )

    halos = [[halo(hop, kind) for kind in range(2)] for hop in range(SPAN)]

    def back(hop, kind):
        return pltpu.make_async_remote_copy(
            src_ref=snd.at[hop, kind],
            dst_ref=rcv.at[hop, kind],
            send_sem=back_send.at[hop, kind],
            recv_sem=back_recv.at[hop, kind],
            device_id=(prv, g),
            device_id_type=MESH,
        )

    backs = [[back(hop, kind) for kind in range(2)] for hop in range(SPAN)]

    docs = doc_ref.shape[1]
    lens = jnp.broadcast_to(doc_ref[...].astype(jnp.float32), (docs, docs))
    upto = lax.broadcasted_iota(jnp.int32, (docs, docs), 1) <= lax.broadcasted_iota(
        jnp.int32, (docs, docs), 0
    )
    ends = jnp.sum(jnp.where(upto, lens, 0.0), axis=1, keepdims=True)
    q_pos = (s * rows + lax.broadcasted_iota(jnp.int32, (1, rows), 1)).astype(jnp.float32)
    begin = jnp.max(jnp.where(ends <= q_pos, ends, 0.0), axis=0, keepdims=True)

    def set_up(w, _):
        k_pos = (
            (s - SPAN + w) * rows + lax.broadcasted_iota(jnp.int32, (rows, rows), 0)
        ).astype(jnp.float32)
        seen = (k_pos >= begin) & (k_pos <= q_pos)
        bias[w] = jnp.where(seen, 0.0, HIDDEN)
        v_t[w, D:, :] = jnp.ones((ONES, rows), jnp.bfloat16)
        part[w] = jnp.zeros(part.shape[1:], jnp.float32)
        return 0

    lax.fori_loop(0, WIN, set_up, 0)

    def clear(c, _):
        max_s[WIN, c] = jnp.full(max_s.shape[2:], HIDDEN, jnp.float32)
        out_t[c] = jnp.zeros(out_t.shape[1:], jnp.float32)
        dq_t[c] = jnp.zeros(dq_t.shape[1:], jnp.float32)
        return 0

    lax.fori_loop(0, chunks, clear, 0)

    def stack(src, dst, c):
        for u in range(pair):
            dst[c, u * rows : (u + 1) * rows, :] = src[:, columns(c * pair + u)]

    locals_[2].wait()

    def set_grad(c, _):
        stack(do_loc, do_s, c)
        do_t[c] = do_s[c].T
        return 0

    lax.fori_loop(0, chunks, set_grad, 0)

    def turn_kv(w):
        k_t[w] = kv[w, 0].T
        v_t[w, :D, :] = kv[w, 1].T

    def pass_on(hop, kind):
        halos[hop - 1][kind].wait_recv()
        halos[hop][kind].start()

    def take_queries(half):
        for copy in sends[2 + half]:
            copy.wait_recv()
        for c in range(per_half):
            stack(q_loc, q_s, half * per_half + c)

    for kind in range(2):
        locals_[kind].wait()
        for copy in sends[kind]:
            copy.wait_recv()
        halos[0][kind].start()
    turn_kv(SPAN)
    for kind in range(2):
        pass_on(1, kind)
    turn_kv(2)
    locals_[3].wait()
    take_queries(0)

    def forward(step, _):
        w, half = SPAN - step // 2, lax.rem(step, 2)

        @pl.when(step == 1)
        def _():
            take_queries(1)
            pass_on(2, 0)

        @pl.when(step == 2)
        def _():
            pass_on(2, 1)
            turn_kv(1)

        @pl.when(step == 2 * SPAN)
        def _():
            for kind in range(2):
                halos[2][kind].wait_recv()
            turn_kv(0)

        mask = jnp.concatenate([bias[w]] * pair, axis=1)
        mine_ = [half * per_half + c for c in range(per_half)]
        scores = [dot_nt(kv[w, 0], q_s[c]) + mask for c in mine_]
        for c, score in zip(mine_, scores):
            old = max_s[w + 1, c]
            top = jnp.maximum(jnp.max(score, axis=0, keepdims=True), old)
            max_s[w, c] = top
            prob = jnp.exp2(score * SCALE_2 - top * SCALE_2)
            prob_s[w, c] = prob
            add = dot(v_t[w], prob.astype(jnp.bfloat16))
            out_t[c] = out_t[c] * jnp.exp2((old - top) * SCALE_2) + add
        return 0

    lax.fori_loop(0, 2 * WIN, forward, 0)

    def finish(c, _):
        inv = 1.0 / out_t[c, D : D + 1, :]
        top = max_s[0, c]
        for w in range(WIN):
            ratio_s[w, c] = jnp.exp2((max_s[w, c] - top) * SCALE_2) * inv
        out = (out_t[c, :D, :] * inv).astype(jnp.bfloat16)
        attn_t[c] = out
        delta_s[c] = jnp.sum(
            out.astype(jnp.float32) * do_t[c].astype(jnp.float32), axis=0, keepdims=True
        )
        return 0

    lax.fori_loop(0, chunks, finish, 0)

    def pass_back(hop):
        for kind in (1, 0):
            total = part[hop, kind] * SCALE if kind == 0 else part[hop, kind]
            if hop > 0:
                backs[hop - 1][kind].wait_recv()
                total = total + rcv[hop - 1, kind].astype(jnp.float32)
            if hop < SPAN:
                snd[hop, kind] = total.astype(jnp.bfloat16)
                backs[hop][kind].start()
            else:
                (dk_ref, dv_ref)[kind][...] = total.astype(jnp.bfloat16)

    def unturn(src, dst, scale):
        def one(c, _):
            for u in range(pair):
                part_ = src[c, :, u * rows : (u + 1) * rows]
                if scale is not None:
                    part_ = (part_ * scale).astype(jnp.bfloat16)
                dst[:, columns(c * pair + u)] = part_.T
            return 0

        lax.fori_loop(0, chunks, one, 0)

    def backward(step, _):
        w, half = step // 2, lax.rem(step, 2)
        mine_ = [half * per_half + c for c in range(per_half)]
        grads = [dot(kv[w, 1], do_t[c]) for c in mine_]
        for c, grad in zip(mine_, grads):
            prob = prob_s[w, c] * ratio_s[w, c]
            ds = (prob * (grad - delta_s[c])).astype(jnp.bfloat16)
            part[w, 1] += dot(prob.astype(jnp.bfloat16), do_s[c])
            part[w, 0] += dot(ds, q_s[c])
            dq_t[c] += dot(k_t[w], ds)

        for hop in range(SPAN):

            @pl.when(step == 2 * hop + 1)
            def _(hop=hop):
                if hop == 1:
                    unturn(attn_t, attn_ref, None)
                pass_back(hop)

        return 0

    lax.fori_loop(0, 2 * WIN, backward, 0)
    unturn(dq_t, dq_ref, SCALE)
    pass_back(SPAN)

    for group in sends + halos + backs:
        for copy in group:
            copy.wait_send()


def settle(*refs):
    n = len(refs) // 2
    copies = [
        pltpu.make_async_copy(refs[i], refs[n + i], refs[-1].at[i]) for i in range(n)
    ]
    for copy in copies:
        copy.start()
    for copy in copies:
        copy.wait()


def per_device(n_seq, n_kvh, query_in, key_in, value_in, grad_out, doc_lengths):
    rows, cols = grad_out.shape
    chunks, wide = cols // (D * PAIR), PAIR * rows
    bf16, f32 = jnp.bfloat16, jnp.float32
    vmem = pl.BlockSpec(memory_space=pltpu.VMEM)
    hbm = pl.BlockSpec(memory_space=pltpu.HBM)
    dma = pltpu.SemaphoreType.DMA
    shapes = (
        jax.ShapeDtypeStruct((rows, cols), bf16),
        jax.ShapeDtypeStruct((rows, cols), bf16),
        jax.ShapeDtypeStruct((rows, D), bf16),
        jax.ShapeDtypeStruct((rows, D), bf16),
    )
    results = pl.pallas_call(
        functools.partial(kernel, n_seq, n_kvh),
        out_shape=tuple(pltpu.VMEM(shape.shape, shape.dtype) for shape in shapes),
        in_specs=[vmem, hbm, hbm, hbm, hbm],
        out_specs=(vmem, vmem, vmem, vmem),
        scratch_shapes=[
            pltpu.VMEM((rows, cols), bf16),
            pltpu.VMEM((rows, cols), bf16),
            pltpu.VMEM((chunks, wide, D), bf16),
            pltpu.VMEM((chunks, wide, D), bf16),
            pltpu.VMEM((chunks, D, wide), bf16),
            pltpu.VMEM((WIN, 2, rows, D), bf16),
            pltpu.VMEM((WIN, D, rows), bf16),
            pltpu.VMEM((WIN, D + ONES, rows), bf16),
            pltpu.VMEM((WIN, rows, rows), f32),
            pltpu.VMEM((WIN, chunks, rows, wide), f32),
            pltpu.VMEM((WIN + 1, chunks, 1, wide), f32),
            pltpu.VMEM((chunks, D + ONES, wide), f32),
            pltpu.VMEM((chunks, D, wide), bf16),
            pltpu.VMEM((chunks, D, wide), f32),
            pltpu.VMEM((WIN, chunks, 1, wide), f32),
            pltpu.VMEM((chunks, 1, wide), f32),
            pltpu.VMEM((WIN, 2, rows, D), f32),
            pltpu.VMEM((SPAN, 2, rows, D), bf16),
            pltpu.VMEM((SPAN, 2, rows, D), bf16),
            dma((4,)),
            dma((4, n_kvh - 1)),
            dma((4, n_kvh - 1)),
            dma((SPAN, 2)),
            dma((SPAN, 2)),
            dma((SPAN, 2)),
            dma((SPAN, 2)),
        ],
        compiler_params=pltpu.CompilerParams(
            collective_id=0, has_side_effects=True, vmem_limit_bytes=48 * 1024 * 1024
        ),
    )(
        *(
            pltpu.with_memory_space_constraint(operand, pltpu.HBM)
            for operand in (doc_lengths.reshape(1, -1), query_in, key_in, value_in, grad_out)
        )
    )
    return pl.pallas_call(
        settle,
        out_shape=shapes,
        in_specs=[vmem] * len(shapes),
        out_specs=(hbm,) * len(shapes),
        scratch_shapes=[dma((len(shapes),))],
    )(*(pltpu.with_memory_space_constraint(result, pltpu.VMEM) for result in results))


def solution(mesh):
    placed = (
        P(("seq", "kvh"), None),
        P(("seq", "kvh"), None),
        P(("seq", "kvh"), None),
        P("seq", "kvh"),
        P(),
    )
    return jax.shard_map(
        functools.partial(per_device, mesh.shape["seq"], mesh.shape["kvh"]),
        mesh=mesh,
        in_specs=placed,
        out_specs=(P("seq", "kvh"), P("seq", "kvh"), P("seq", "kvh"), P("seq", "kvh")),
        check_vma=False,
    )
```

time: 160 us -> 47.8 us (0.30)
  the two profiles are of different devices: /device:TPU:2 before, /device:TPU:8 now
where the time goes in v1:
time: 47.8 us; the launch traced here: 47.6 us
  Pallas kernels  47 us (98%)
  between operations  0.64 us (1%)
    pallas_call x1, Pallas kernels, per_device(): pl.pallas_call(functools.partial(kernel, n_seq, n_kvh), out_shape=tuple((...  46 us
    pallas_call x1, Pallas kernels, per_device(): pl.pallas_call(settle, out_shape=shapes, in_specs=[vmem] * len(shapes), o...  1.03 us

profile of v1, /device:TPU:8, one launch (start us, length us, event | category | flops | bytes accessed | tf_op | source)
XLA Modules:
  0.0 47.6 jit_solution(15726945622136519365)
XLA Ops:
  0.6 46.0 %shard_map.84 = (bf16[256,1024]{1,0:T(8,128)(2,1)S(1)}, bf16[256,1024]{1,0:T(8,128)(2,1)S(1)}, bf16[256,128]{1,0:T(8,128)(2,1)S(1)}, bf16[256,128]{1,0:T(8,128)(2,1)S(1)}) custom-call(s32[1,64]{1,0:T(1,128)} %bitcast.1, bf16[32,8192]{1,0:T(8,128)(2,1)} %q_hbm.1, bf16[32,1024]{1,0:T(8,128)(2,1)} %k_hbm.1, bf16[32,1024]{1,0:T(8,128)(2,1)} %v_hbm.1, ...), custom_call_target="tpu_custom_call" | custom-call | tf_op jit(solution)/shard_map/pallas_call | solution.py:340
  46.6 1.0 %shard_map.85 = (bf16[256,1024]{1,0:T(8,128)(2,1)}, bf16[256,1024]{1,0:T(8,128)(2,1)}, bf16[256,128]{1,0:T(8,128)(2,1)}, bf16[256,128]{1,0:T(8,128)(2,1)}) custom-call(bf16[256,1024]{1,0:T(8,128)(2,1)S(1)} %get-tuple-element.8.refs_0_, bf16[256,1024]{1,0:T(8,128)(2,1)S(1)} %get-tuple-element.9.refs_1_, bf16[256,128]{1,0:T(8,128)(2,1)S(1)} %get-tuple-element.10.refs_2_, ...), custom_call_target="tpu_custom_call" | custom-call | tf_op jit(solution)/shard_map/pallas_call | solution.py:382

commit v2 on v1

--- a/solution.py
+++ b/solution.py
@@ -21,10 +21,6 @@
 
 def dot(a, b):
     return jnp.dot(a, b, preferred_element_type=jnp.float32)
-
-
-def dot_nt(a, b):
-    return lax.dot_general(a, b, (((1,), (1,)), ((), ())), preferred_element_type=jnp.float32)
 
 
 def kernel(
@@ -42,6 +38,7 @@
     q_loc,
     do_loc,
     q_s,
+    q_t,
     do_s,
     do_t,
     kv,
@@ -116,8 +113,9 @@
         )
 
     sends = [[to_peer(kind, j) for j in range(1, n_kvh)] for kind in range(4)]
-    for kind in range(4):
-        for copy in sends[kind]:
+
+    def start(copies):
+        for copy in copies:
             copy.start()
 
     def halo(hop, kind):
@@ -144,48 +142,10 @@
 
     backs = [[back(hop, kind) for kind in range(2)] for hop in range(SPAN)]
 
-    docs = doc_ref.shape[1]
-    lens = jnp.broadcast_to(doc_ref[...].astype(jnp.float32), (docs, docs))
-    upto = lax.broadcasted_iota(jnp.int32, (docs, docs), 1) <= lax.broadcasted_iota(
-        jnp.int32, (docs, docs), 0
-    )
-    ends = jnp.sum(jnp.where(upto, lens, 0.0), axis=1, keepdims=True)
-    q_pos = (s * rows + lax.broadcasted_iota(jnp.int32, (1, rows), 1)).astype(jnp.float32)
-    begin = jnp.max(jnp.where(ends <= q_pos, ends, 0.0), axis=0, keepdims=True)
-
-    def set_up(w, _):
-        k_pos = (
-            (s - SPAN + w) * rows + lax.broadcasted_iota(jnp.int32, (rows, rows), 0)
-        ).astype(jnp.float32)
-        seen = (k_pos >= begin) & (k_pos <= q_pos)
-        bias[w] = jnp.where(seen, 0.0, HIDDEN)
-        v_t[w, D:, :] = jnp.ones((ONES, rows), jnp.bfloat16)
-        part[w] = jnp.zeros(part.shape[1:], jnp.float32)
-        return 0
-
-    lax.fori_loop(0, WIN, set_up, 0)
-
-    def clear(c, _):
-        max_s[WIN, c] = jnp.full(max_s.shape[2:], HIDDEN, jnp.float32)
-        out_t[c] = jnp.zeros(out_t.shape[1:], jnp.float32)
-        dq_t[c] = jnp.zeros(dq_t.shape[1:], jnp.float32)
-        return 0
-
-    lax.fori_loop(0, chunks, clear, 0)
-
     def stack(src, dst, c):
         for u in range(pair):
             dst[c, u * rows : (u + 1) * rows, :] = src[:, columns(c * pair + u)]
 
-    locals_[2].wait()
-
-    def set_grad(c, _):
-        stack(do_loc, do_s, c)
-        do_t[c] = do_s[c].T
-        return 0
-
-    lax.fori_loop(0, chunks, set_grad, 0)
-
     def turn_kv(w):
         k_t[w] = kv[w, 0].T
         v_t[w, :D, :] = kv[w, 1].T
@@ -197,54 +157,141 @@
     def take_queries(half):
         for copy in sends[2 + half]:
             copy.wait_recv()
-        for c in range(per_half):
-            stack(q_loc, q_s, half * per_half + c)
-
+        for c in range(half * per_half, (half + 1) * per_half):
+            stack(q_loc, q_s, c)
+            q_t[c] = q_s[c].T
+
+    def set_all():
+        docs = doc_ref.shape[1]
+        lens = jnp.broadcast_to(doc_ref[...].astype(jnp.float32), (docs, docs))
+        upto = lax.broadcasted_iota(jnp.int32, (docs, docs), 1) <= lax.broadcasted_iota(
+            jnp.int32, (docs, docs), 0
+        )
+        ends = jnp.sum(jnp.where(upto, lens, 0.0), axis=1, keepdims=True)
+        q_pos = (s * rows + lax.broadcasted_iota(jnp.int32, (1, rows), 1)).astype(jnp.float32)
+        begin = jnp.max(jnp.where(ends <= q_pos, ends, 0.0), axis=0, keepdims=True)
+
+        def set_up(w, _):
+            k_pos = (
+                (s - SPAN + w) * rows + lax.broadcasted_iota(jnp.int32, (rows, rows), 0)
+            ).astype(jnp.float32)
+            seen = (k_pos >= begin) & (k_pos <= q_pos)
+            bias[w] = jnp.where(seen, 0.0, HIDDEN)
+            v_t[w, D:, :] = jnp.ones((ONES, rows), jnp.bfloat16)
+            part[w] = jnp.zeros(part.shape[1:], jnp.float32)
+            return 0
+
+        lax.fori_loop(0, WIN, set_up, 0)
+
+        def clear(c, _):
+            max_s[WIN, c] = jnp.full(max_s.shape[2:], HIDDEN, jnp.float32)
+            out_t[c] = jnp.zeros(out_t.shape[1:], jnp.float32)
+            dq_t[c] = jnp.zeros(dq_t.shape[1:], jnp.float32)
+            return 0
+
+        lax.fori_loop(0, chunks, clear, 0)
+
+        locals_[2].wait()
+
+        def set_grad(c, _):
+            stack(do_loc, do_s, c)
+            do_t[c] = do_s[c].T
+            return 0
+
+        lax.fori_loop(0, chunks, set_grad, 0)
+
+    def piece_on(kind, j):
+        place = (
+            pl.ds(pl.multiple_of(lax.rem(g + n_kvh - j, n_kvh) * piece, piece), piece),
+            slice(None),
+        )
+        pltpu.make_async_remote_copy(
+            src_ref=kv.at[(SPAN, kind) + place],
+            dst_ref=kv.at[(SPAN - 1, kind) + place],
+            send_sem=halo_send.at[0, kind],
+            recv_sem=halo_recv.at[0, kind],
+            device_id=(nxt, g),
+            device_id_type=MESH,
+        ).start()
+
+    near_first = sorted(range(1, n_kvh), key=lambda j: min(j, n_kvh - j))
+    for kind in range(2):
+        start(sends[kind])
     for kind in range(2):
         locals_[kind].wait()
-        for copy in sends[kind]:
-            copy.wait_recv()
-        halos[0][kind].start()
+        piece_on(kind, 0)
+    for kind in range(2):
+        for j in near_first:
+            sends[kind][j - 1].wait_recv()
+            piece_on(kind, j)
+        start(sends[2 + kind])
+
+    set_all()
     turn_kv(SPAN)
-    for kind in range(2):
-        pass_on(1, kind)
-    turn_kv(2)
+    pass_on(1, 0)
+    pass_on(1, 1)
+    turn_kv(SPAN - 1)
+    pass_on(2, 0)
     locals_[3].wait()
     take_queries(0)
 
+    def weigh(w, c, score):
+        old = max_s[w + 1, c]
+        top = jnp.maximum(jnp.max(score, axis=0, keepdims=True), old)
+        max_s[w, c] = top
+        prob = jnp.exp2(score * SCALE_2 - top * SCALE_2)
+        prob_s[w, c] = prob
+        return prob
+
+    def gather(w, c, prob):
+        shrink = jnp.exp2((max_s[w + 1, c] - max_s[w, c]) * SCALE_2)
+        out_t[c] = out_t[c] * shrink + dot(v_t[w], prob.astype(jnp.bfloat16))
+
+    def chunks_of(half):
+        return [half * per_half + c for c in range(per_half)]
+
+    def scores(w, half):
+        mask = jnp.concatenate([bias[w]] * pair, axis=1)
+        return [dot(kv[w, 0], q_t[c]) + mask for c in chunks_of(half)]
+
     def forward(step, _):
-        w, half = SPAN - step // 2, lax.rem(step, 2)
+        early = 1 - step // 4
+        w = SPAN - early * lax.rem(step, 2) - (1 - early) * 2
+        half = early * (step // 2) + (1 - early) * lax.rem(step, 2)
 
         @pl.when(step == 1)
         def _():
-            take_queries(1)
-            pass_on(2, 0)
+            pass_on(2, 1)
 
         @pl.when(step == 2)
         def _():
-            pass_on(2, 1)
+            take_queries(1)
+
+        @pl.when(step == 4)
+        def _():
             turn_kv(1)
 
-        @pl.when(step == 2 * SPAN)
-        def _():
-            for kind in range(2):
-                halos[2][kind].wait_recv()
-            turn_kv(0)
-
-        mask = jnp.concatenate([bias[w]] * pair, axis=1)
-        mine_ = [half * per_half + c for c in range(per_half)]
-        scores = [dot_nt(kv[w, 0], q_s[c]) + mask for c in mine_]
-        for c, score in zip(mine_, scores):
-            old = max_s[w + 1, c]
-            top = jnp.maximum(jnp.max(score, axis=0, keepdims=True), old)
-            max_s[w, c] = top
-            prob = jnp.exp2(score * SCALE_2 - top * SCALE_2)
-            prob_s[w, c] = prob
-            add = dot(v_t[w], prob.astype(jnp.bfloat16))
-            out_t[c] = out_t[c] * jnp.exp2((old - top) * SCALE_2) + add
-        return 0
-
-    lax.fori_loop(0, 2 * WIN, forward, 0)
+        for c, score in zip(chunks_of(half), scores(w, half)):
+            gather(w, c, weigh(w, c, score))
+        return 0
+
+    lax.fori_loop(0, 6, forward, 0)
+
+    def oldest_scores(half, _):
+        for c, score in zip(chunks_of(half), scores(0, half)):
+            weigh(0, c, score)
+        return 0
+
+    halos[2][0].wait_recv()
+    lax.fori_loop(0, 2, oldest_scores, 0)
+    halos[2][1].wait_recv()
+    turn_kv(0)
+
+    def oldest_sum(c, _):
+        gather(0, c, prob_s[0, c])
+        return 0
+
+    lax.fori_loop(0, chunks, oldest_sum, 0)
 
     def finish(c, _):
         inv = 1.0 / out_t[c, D : D + 1, :]
@@ -260,8 +307,8 @@
 
     lax.fori_loop(0, chunks, finish, 0)
 
-    def pass_back(hop):
-        for kind in (1, 0):
+    def pass_back(hop, kinds=(1, 0)):
+        for kind in kinds:
             total = part[hop, kind] * SCALE if kind == 0 else part[hop, kind]
             if hop > 0:
                 backs[hop - 1][kind].wait_recv()
@@ -283,18 +330,39 @@
 
         lax.fori_loop(0, chunks, one, 0)
 
+    def one_dv(w, c, prob):
+        part[w, 1] += dot(prob.astype(jnp.bfloat16), do_s[c])
+
+    def one_dk(w, c, prob, grad):
+        ds = (prob * (grad - delta_s[c])).astype(jnp.bfloat16)
+        part[w, 0] += dot(ds, q_s[c])
+        dq_t[c] += dot(k_t[w], ds)
+
+    def oldest_dv(half, _):
+        for c in chunks_of(half):
+            one_dv(0, c, prob_s[0, c] * ratio_s[0, c])
+        return 0
+
+    def oldest_dk(half, _):
+        grads = [dot(kv[0, 1], do_t[c]) for c in chunks_of(half)]
+        for c, grad in zip(chunks_of(half), grads):
+            one_dk(0, c, prob_s[0, c] * ratio_s[0, c], grad)
+        return 0
+
+    lax.fori_loop(0, 2, oldest_dv, 0)
+    pass_back(0, (1,))
+    lax.fori_loop(0, 2, oldest_dk, 0)
+    pass_back(0, (0,))
+
     def backward(step, _):
         w, half = step // 2, lax.rem(step, 2)
-        mine_ = [half * per_half + c for c in range(per_half)]
-        grads = [dot(kv[w, 1], do_t[c]) for c in mine_]
-        for c, grad in zip(mine_, grads):
+        grads = [dot(kv[w, 1], do_t[c]) for c in chunks_of(half)]
+        for c, grad in zip(chunks_of(half), grads):
             prob = prob_s[w, c] * ratio_s[w, c]
-            ds = (prob * (grad - delta_s[c])).astype(jnp.bfloat16)
-            part[w, 1] += dot(prob.astype(jnp.bfloat16), do_s[c])
-            part[w, 0] += dot(ds, q_s[c])
-            dq_t[c] += dot(k_t[w], ds)
-
-        for hop in range(SPAN):
+            one_dv(w, c, prob)
+            one_dk(w, c, prob, grad)
+
+        for hop in range(1, SPAN):
 
             @pl.when(step == 2 * hop + 1)
             def _(hop=hop):
@@ -304,7 +372,7 @@
 
         return 0
 
-    lax.fori_loop(0, 2 * WIN, backward, 0)
+    lax.fori_loop(2, 2 * WIN, backward, 0)
     unturn(dq_t, dq_ref, SCALE)
     pass_back(SPAN)
 
@@ -346,6 +414,7 @@
             pltpu.VMEM((rows, cols), bf16),
             pltpu.VMEM((rows, cols), bf16),
             pltpu.VMEM((chunks, wide, D), bf16),
+            pltpu.VMEM((chunks, D, wide), bf16),
             pltpu.VMEM((chunks, wide, D), bf16),
             pltpu.VMEM((chunks, D, wide), bf16),
             pltpu.VMEM((WIN, 2, rows, D), bf16),

time: 47.8 us -> 45.7 us (0.956)
  Pallas kernels: 47 us -> 44.9 us
    pallas_call x1, Pallas kernels: 46 us -> 43.9 us  [per_device(): pl.pallas_call(functools.partial(kernel, n_seq, n_kvh), out_shape=tuple((...]
where the time goes in v2:
time: 45.7 us; the launch traced here: 45.6 us
  Pallas kernels  44.9 us (98%)
  between operations  0.64 us (1%)
    pallas_call x1, Pallas kernels, per_device(): pl.pallas_call(functools.partial(kernel, n_seq, n_kvh), out_shape=tuple((...  43.9 us
    pallas_call x1, Pallas kernels, per_device(): pl.pallas_call(settle, out_shape=shapes, in_specs=[vmem] * len(shapes), o...  1.03 us

profile of v2, /device:TPU:8, one launch (start us, length us, event | category | flops | bytes accessed | tf_op | source)
XLA Modules:
  0.0 45.6 jit_solution(16427407797270950566)
XLA Ops:
  0.6 43.9 %shard_map.84 = (bf16[256,1024]{1,0:T(8,128)(2,1)S(1)}, bf16[256,1024]{1,0:T(8,128)(2,1)S(1)}, bf16[256,128]{1,0:T(8,128)(2,1)S(1)}, bf16[256,128]{1,0:T(8,128)(2,1)S(1)}) custom-call(s32[1,64]{1,0:T(1,128)} %bitcast.1, bf16[32,8192]{1,0:T(8,128)(2,1)} %q_hbm.1, bf16[32,1024]{1,0:T(8,128)(2,1)} %k_hbm.1, bf16[32,1024]{1,0:T(8,128)(2,1)} %v_hbm.1, ...), custom_call_target="tpu_custom_call" | custom-call | tf_op jit(solution)/shard_map/pallas_call | solution.py:408
  44.5 1.0 %shard_map.85 = (bf16[256,1024]{1,0:T(8,128)(2,1)}, bf16[256,1024]{1,0:T(8,128)(2,1)}, bf16[256,128]{1,0:T(8,128)(2,1)}, bf16[256,128]{1,0:T(8,128)(2,1)}) custom-call(bf16[256,1024]{1,0:T(8,128)(2,1)S(1)} %get-tuple-element.8.refs_0_, bf16[256,1024]{1,0:T(8,128)(2,1)S(1)} %get-tuple-element.9.refs_1_, bf16[256,128]{1,0:T(8,128)(2,1)S(1)} %get-tuple-element.10.refs_2_, ...), custom_call_target="tpu_custom_call" | custom-call | tf_op jit(solution)/shard_map/pallas_call | solution.py:451

commit v3 on v2

--- a/solution.py
+++ b/solution.py
@@ -21,6 +21,10 @@
 
 def dot(a, b):
     return jnp.dot(a, b, preferred_element_type=jnp.float32)
+
+
+def dot_nt(a, b):
+    return lax.dot_general(a, b, (((1,), (1,)), ((), ())), preferred_element_type=jnp.float32)
 
 
 def kernel(
@@ -37,9 +41,7 @@
     dv_ref,
     q_loc,
     do_loc,
-    q_s,
     q_t,
-    do_s,
     do_t,
     kv,
     k_t,
@@ -64,7 +66,7 @@
     back_recv,
 ):
     rows, cols = do_loc.shape
-    chunks, wide = q_s.shape[0], q_s.shape[1]
+    chunks, wide = q_t.shape[0], q_t.shape[2]
     pair = wide // rows
     per_half = chunks // 2
     piece = q_hbm.shape[0]
@@ -142,9 +144,9 @@
 
     backs = [[back(hop, kind) for kind in range(2)] for hop in range(SPAN)]
 
-    def stack(src, dst, c):
+    def turn(src, dst, c):
         for u in range(pair):
-            dst[c, u * rows : (u + 1) * rows, :] = src[:, columns(c * pair + u)]
+            dst[c, :, u * rows : (u + 1) * rows] = src[:, columns(c * pair + u)].T
 
     def turn_kv(w):
         k_t[w] = kv[w, 0].T
@@ -158,8 +160,7 @@
         for copy in sends[2 + half]:
             copy.wait_recv()
         for c in range(half * per_half, (half + 1) * per_half):
-            stack(q_loc, q_s, c)
-            q_t[c] = q_s[c].T
+            turn(q_loc, q_t, c)
 
     def set_all():
         docs = doc_ref.shape[1]
@@ -194,8 +195,7 @@
         locals_[2].wait()
 
         def set_grad(c, _):
-            stack(do_loc, do_s, c)
-            do_t[c] = do_s[c].T
+            turn(do_loc, do_t, c)
             return 0
 
         lax.fori_loop(0, chunks, set_grad, 0)
@@ -220,11 +220,12 @@
     for kind in range(2):
         locals_[kind].wait()
         piece_on(kind, 0)
+    for kind in range(2, 4):
+        start(sends[kind])
     for kind in range(2):
         for j in near_first:
             sends[kind][j - 1].wait_recv()
             piece_on(kind, j)
-        start(sends[2 + kind])
 
     set_all()
     turn_kv(SPAN)
@@ -317,7 +318,7 @@
                 snd[hop, kind] = total.astype(jnp.bfloat16)
                 backs[hop][kind].start()
             else:
-                (dk_ref, dv_ref)[kind][...] = total.astype(jnp.bfloat16)
+                (dk_ref, dv_ref)[kind][...] = total.astype(jnp.bfloat16).T
 
     def unturn(src, dst, scale):
         def one(c, _):
@@ -331,11 +332,11 @@
         lax.fori_loop(0, chunks, one, 0)
 
     def one_dv(w, c, prob):
-        part[w, 1] += dot(prob.astype(jnp.bfloat16), do_s[c])
+        part[w, 1] += dot_nt(do_t[c], prob.astype(jnp.bfloat16))
 
     def one_dk(w, c, prob, grad):
         ds = (prob * (grad - delta_s[c])).astype(jnp.bfloat16)
-        part[w, 0] += dot(ds, q_s[c])
+        part[w, 0] += dot_nt(q_t[c], ds)
         dq_t[c] += dot(k_t[w], ds)
 
     def oldest_dv(half, _):
@@ -413,9 +414,7 @@
         scratch_shapes=[
             pltpu.VMEM((rows, cols), bf16),
             pltpu.VMEM((rows, cols), bf16),
-            pltpu.VMEM((chunks, wide, D), bf16),
             pltpu.VMEM((chunks, D, wide), bf16),
-            pltpu.VMEM((chunks, wide, D), bf16),
             pltpu.VMEM((chunks, D, wide), bf16),
             pltpu.VMEM((WIN, 2, rows, D), bf16),
             pltpu.VMEM((WIN, D, rows), bf16),
@@ -428,9 +427,9 @@
             pltpu.VMEM((chunks, D, wide), f32),
             pltpu.VMEM((WIN, chunks, 1, wide), f32),
             pltpu.VMEM((chunks, 1, wide), f32),
-            pltpu.VMEM((WIN, 2, rows, D), f32),
-            pltpu.VMEM((SPAN, 2, rows, D), bf16),
-            pltpu.VMEM((SPAN, 2, rows, D), bf16),
+            pltpu.VMEM((WIN, 2, D, rows), f32),
+            pltpu.VMEM((SPAN, 2, D, rows), bf16),
+            pltpu.VMEM((SPAN, 2, D, rows), bf16),
             dma((4,)),
             dma((4, n_kvh - 1)),
             dma((4, n_kvh - 1)),

time: 45.7 us -> 46.2 us (1.011)
  Pallas kernels: 44.9 us -> 45.5 us
    pallas_call x1, Pallas kernels: 43.9 us -> 44.4 us  [per_device(): pl.pallas_call(functools.partial(kernel, n_seq, n_kvh), out_shape=tuple((...]
where the time goes in v3:
time: 46.2 us; the launch traced here: 46.1 us
  Pallas kernels  45.5 us (98%)
  between operations  0.64 us (1%)
    pallas_call x1, Pallas kernels, per_device(): pl.pallas_call(functools.partial(kernel, n_seq, n_kvh), out_shape=tuple((...  44.4 us
    pallas_call x1, Pallas kernels, per_device(): pl.pallas_call(settle, out_shape=shapes, in_specs=[vmem] * len(shapes), o...  1.03 us

profile of v3, /device:TPU:8, one launch (start us, length us, event | category | flops | bytes accessed | tf_op | source)
XLA Modules:
  0.0 46.1 jit_solution(1353958414802403962)
XLA Ops:
  0.6 44.4 %shard_map.84 = (bf16[256,1024]{1,0:T(8,128)(2,1)S(1)}, bf16[256,1024]{1,0:T(8,128)(2,1)S(1)}, bf16[256,128]{1,0:T(8,128)(2,1)S(1)}, bf16[256,128]{1,0:T(8,128)(2,1)S(1)}) custom-call(s32[1,64]{1,0:T(1,128)} %bitcast.1, bf16[32,8192]{1,0:T(8,128)(2,1)} %q_hbm.1, bf16[32,1024]{1,0:T(8,128)(2,1)} %k_hbm.1, bf16[32,1024]{1,0:T(8,128)(2,1)} %v_hbm.1, ...), custom_call_target="tpu_custom_call" | custom-call | tf_op jit(solution)/shard_map/pallas_call | solution.py:409
  45.1 1.0 %shard_map.85 = (bf16[256,1024]{1,0:T(8,128)(2,1)}, bf16[256,1024]{1,0:T(8,128)(2,1)}, bf16[256,128]{1,0:T(8,128)(2,1)}, bf16[256,128]{1,0:T(8,128)(2,1)}) custom-call(bf16[256,1024]{1,0:T(8,128)(2,1)S(1)} %get-tuple-element.8.refs_0_, bf16[256,1024]{1,0:T(8,128)(2,1)S(1)} %get-tuple-element.9.refs_1_, bf16[256,128]{1,0:T(8,128)(2,1)S(1)} %get-tuple-element.10.refs_2_, ...), custom_call_target="tpu_custom_call" | custom-call | tf_op jit(solution)/shard_map/pallas_call | solution.py:450

commit v4 on v3

v4 whole, which is shorter than its diff:
```python
import functools
import math

import jax
import jax.numpy as jnp
from jax import lax
from jax.experimental import pallas as pl
from jax.experimental.pallas import tpu as pltpu
from jax.sharding import PartitionSpec as P

MESH = pl.DeviceIdType.MESH
D = 128
SPAN = 3
WIN = SPAN + 1
HIDDEN = -1e30
SCALE = 1.0 / math.sqrt(D)
SCALE_2 = SCALE * math.log2(math.e)
PAIR = 2


def dot(a, b):
    return jnp.dot(a, b, preferred_element_type=jnp.float32)


def dot_nt(a, b):
    return lax.dot_general(a, b, (((1,), (1,)), ((), ())), preferred_element_type=jnp.float32)


def kernel(
    n_seq,
    n_kvh,
    doc_ref,
    q_hbm,
    k_hbm,
    v_hbm,
    do_hbm,
    attn_ref,
    dq_ref,
    dk_ref,
    dv_ref,
    q_loc,
    do_loc,
    q_t,
    do_t,
    kv,
    k_t,
    v_t,
    bias,
    prob_s,
    max_s,
    sum_s,
    out_t,
    attn_t,
    dq_t,
    ratio_s,
    delta_s,
    part,
    snd,
    rcv,
    local_sem,
    a2a_send,
    a2a_recv,
    halo_send,
    halo_recv,
    back_send,
    back_recv,
):
    rows, cols = do_loc.shape
    chunks, wide = q_t.shape[0], q_t.shape[2]
    pair = wide // rows
    per_half = chunks // 2
    piece = q_hbm.shape[0]
    s, g = lax.axis_index("seq"), lax.axis_index("kvh")
    nxt, prv = lax.rem(s + 1, n_seq), lax.rem(s + n_seq - 1, n_seq)

    def columns(h, width=D):
        return pl.ds(pl.multiple_of(h * width, width), width)

    mine = pl.ds(pl.multiple_of(g * piece, piece), piece)

    locals_ = [
        pltpu.make_async_copy(k_hbm.at[:, columns(g)], kv.at[SPAN, 0, mine, :], local_sem.at[0]),
        pltpu.make_async_copy(v_hbm.at[:, columns(g)], kv.at[SPAN, 1, mine, :], local_sem.at[1]),
        pltpu.make_async_copy(do_hbm, do_loc, local_sem.at[2]),
        pltpu.make_async_copy(q_hbm.at[:, columns(g, cols)], q_loc.at[mine, :], local_sem.at[3]),
    ]
    for copy in locals_:
        copy.start()

    barrier = pltpu.get_barrier_semaphore()
    for j in range(1, n_kvh):
        pl.semaphore_signal(
            barrier, inc=1, device_id=(s, lax.rem(g + j, n_kvh)), device_id_type=MESH
        )
    for to in (nxt, prv):
        pl.semaphore_signal(barrier, inc=1, device_id=(to, g), device_id_type=MESH)
    pl.semaphore_wait(barrier, n_kvh + 1)

    def to_peer(kind, j):
        peer = lax.rem(g + j, n_kvh)
        if kind >= 2:
            half = cols // 2
            src = q_hbm.at[:, columns(2 * peer + kind - 2, half)]
            dst = q_loc.at[mine, pl.ds((kind - 2) * half, half)]
        else:
            src = (k_hbm, v_hbm)[kind].at[:, columns(peer)]
            dst = kv.at[SPAN, kind, mine, :]
        return pltpu.make_async_remote_copy(
            src_ref=src,
            dst_ref=dst,
            send_sem=a2a_send.at[kind, j - 1],
            recv_sem=a2a_recv.at[kind, j - 1],
            device_id=(s, peer),
            device_id_type=MESH,
        )

    sends = [[to_peer(kind, j) for j in range(1, n_kvh)] for kind in range(4)]
    half_rows = rows // 2

    def halo(hop, kind, part_):
        place = (kind, pl.ds(part_ * half_rows, half_rows), slice(None))
        return pltpu.make_async_remote_copy(
            src_ref=kv.at[(SPAN - hop,) + place],
            dst_ref=kv.at[(SPAN - hop - 1,) + place],
            send_sem=halo_send.at[hop, kind, part_],
            recv_sem=halo_recv.at[hop, kind, part_],
            device_id=(nxt, g),
            device_id_type=MESH,
        )

    halos = [
        [[halo(hop, kind, part_) for part_ in range(2)] for kind in range(2)]
        for hop in range(SPAN)
    ]

    def back(hop, kind, part_):
        return pltpu.make_async_remote_copy(
            src_ref=snd.at[hop, kind, part_],
            dst_ref=rcv.at[hop, kind, part_],
            send_sem=back_send.at[hop, kind, part_],
            recv_sem=back_recv.at[hop, kind, part_],
            device_id=(prv, g),
            device_id_type=MESH,
        )

    backs = [
        [[back(hop, kind, part_) for part_ in range(2)] for kind in range(2)]
        for hop in range(SPAN)
    ]

    def set_mask():
        docs = doc_ref.shape[1]
        lens = jnp.broadcast_to(doc_ref[...].astype(jnp.float32), (docs, docs))
        upto = lax.broadcasted_iota(jnp.int32, (docs, docs), 1) <= lax.broadcasted_iota(
            jnp.int32, (docs, docs), 0
        )
        ends = jnp.sum(jnp.where(upto, lens, 0.0), axis=1, keepdims=True)
        q_pos = (s * rows + lax.broadcasted_iota(jnp.int32, (1, rows), 1)).astype(jnp.float32)
        begin = jnp.max(jnp.where(ends <= q_pos, ends, 0.0), axis=0, keepdims=True)

        def one_block(w, _):
            k_pos = (
                (s - SPAN + w) * rows + lax.broadcasted_iota(jnp.int32, (rows, rows), 0)
            ).astype(jnp.float32)
            seen = (k_pos >= begin) & (k_pos <= q_pos)
            bias[w] = jnp.where(seen, 0.0, HIDDEN)
            part[w] = jnp.zeros(part.shape[1:], jnp.float32)
            return 0

        lax.fori_loop(0, WIN, one_block, 0)

        def clear(c, _):
            max_s[WIN, c] = jnp.full(max_s.shape[2:], HIDDEN, jnp.float32)
            out_t[c] = jnp.zeros(out_t.shape[1:], jnp.float32)
            dq_t[c] = jnp.zeros(dq_t.shape[1:], jnp.float32)
            return 0

        lax.fori_loop(0, chunks, clear, 0)

    def turn(src, dst, c):
        for u in range(pair):
            dst[c, :, u * rows : (u + 1) * rows] = src[:, columns(c * pair + u)].T

    def take_queries(half):
        for copy in sends[2 + half]:
            copy.wait_recv()
        for c in range(half * per_half, (half + 1) * per_half):
            turn(q_loc, q_t, c)

    def piece_on(kind, j):
        source = lax.rem(g + n_kvh - j, n_kvh)
        part_ = source // (n_kvh // 2)
        place = (kind, pl.ds(pl.multiple_of(source * piece, piece), piece), slice(None))
        pltpu.make_async_remote_copy(
            src_ref=kv.at[(SPAN,) + place],
            dst_ref=kv.at[(SPAN - 1,) + place],
            send_sem=halo_send.at[0, kind, part_],
            recv_sem=halo_recv.at[0, kind, part_],
            device_id=(nxt, g),
            device_id_type=MESH,
        ).start()

    near_first = sorted(range(1, n_kvh), key=lambda j: min(j, n_kvh - j))

    def pieces_on(kind):
        for j in near_first:
            sends[kind][j - 1].wait_recv()
            piece_on(kind, j)

    def pass_on(hop, kind):
        for part_ in range(2):
            halos[hop - 1][kind][part_].wait_recv()
            if hop < SPAN:
                halos[hop][kind][part_].start()

    for copy in sends[0]:
        copy.start()
    locals_[0].wait()
    piece_on(0, 0)
    for kind in range(1, 4):
        for copy in sends[kind]:
            copy.start()
    set_mask()

    pieces_on(0)
    pass_on(1, 0)
    pass_on(2, 0)
    locals_[1].wait()
    piece_on(1, 0)
    pieces_on(1)

    locals_[2].wait()

    def turn_grad(c, _):
        turn(do_loc, do_t, c)
        return 0

    lax.fori_loop(0, chunks, turn_grad, 0)

    def turn_k(w, _):
        k_t[w] = kv[w, 0].T
        return 0

    lax.fori_loop(1, WIN, turn_k, 0)
    v_t[SPAN] = kv[SPAN, 1].T
    locals_[3].wait()
    take_queries(0)

    def chunks_of(half):
        return [half * per_half + c for c in range(per_half)]

    def weigh(step, _):
        early = 1 - step // 4
        w = SPAN - early * lax.rem(step, 2) - (1 - early) * (step // 2)
        half = early * (step // 2) + (1 - early) * lax.rem(step, 2)

        @pl.when(step == 2)
        def _():
            take_queries(1)

        @pl.when(step == 5)
        def _():
            pass_on(1, 1)

        @pl.when(step == 6)
        def _():
            pass_on(SPAN, 0)

        mask = jnp.concatenate([bias[w]] * pair, axis=1)
        scores = [dot(kv[w, 0], q_t[c]) + mask for c in chunks_of(half)]
        for c, score in zip(chunks_of(half), scores):
            top = jnp.maximum(jnp.max(score, axis=0, keepdims=True), max_s[w + 1, c])
            max_s[w, c] = top
            prob = jnp.exp2(score * SCALE_2 - top * SCALE_2)
            prob_s[w, c] = prob
            sum_s[w, c] = jnp.sum(prob, axis=0, keepdims=True)
        return 0

    lax.fori_loop(0, 2 * WIN, weigh, 0)

    def even_out(c, _):
        shares = [jnp.exp2((max_s[w, c] - max_s[0, c]) * SCALE_2) for w in range(WIN)]
        inv = 1.0 / sum(shares[w] * sum_s[w, c] for w in range(WIN))
        for w in range(WIN):
            ratio_s[w, c] = shares[w] * inv
        return 0

    lax.fori_loop(0, chunks, even_out, 0)

    def pass_back(hop, kind):
        for part_ in range(2):
            here = slice(part_ * half_rows, (part_ + 1) * half_rows)
            total = part[hop, kind, :, here]
            if kind == 0:
                total = total * SCALE
            if hop > 0:
                backs[hop - 1][kind][part_].wait_recv()
                total = total + rcv[hop - 1, kind, part_].astype(jnp.float32)
            total = total.astype(jnp.bfloat16)
            if hop < SPAN:
                snd[hop, kind, part_] = total
                backs[hop][kind][part_].start()
            else:
                (dk_ref, dv_ref)[kind][here, :] = total.T

    def prob_of(w, c):
        return prob_s[w, c] * ratio_s[w, c]

    def oldest_dv(half, _):
        for c in chunks_of(half):
            part[0, 1] += dot_nt(do_t[c], prob_of(0, c).astype(jnp.bfloat16))
        return 0

    lax.fori_loop(0, 2, oldest_dv, 0)
    pass_back(0, 1)
    pass_on(2, 1)
    for w in (2, 1):
        v_t[w] = kv[w, 1].T

    def values(step, _):
        w, half = step // 2, lax.rem(step, 2)
        for c in chunks_of(half):
            prob = prob_of(w, c).astype(jnp.bfloat16)
            part[w, 1] += dot_nt(do_t[c], prob)
            out_t[c] += dot(v_t[w], prob)

        @pl.when(step == 5)
        def _():
            pass_back(1, 1)

        return 0

    lax.fori_loop(2, 2 * WIN, values, 0)
    pass_on(SPAN, 1)
    v_t[0] = kv[0, 1].T
    k_t[0] = kv[0, 0].T

    def finish(half, _):
        for c in chunks_of(half):
            out = out_t[c] + dot(v_t[0], prob_of(0, c).astype(jnp.bfloat16))
            out = out.astype(jnp.bfloat16)
            attn_t[c] = out
            delta_s[c] = jnp.sum(
                out.astype(jnp.float32) * do_t[c].astype(jnp.float32), axis=0, keepdims=True
            )
        return 0

    lax.fori_loop(0, 2, finish, 0)

    def unturn(src, dst, scale):
        def one(c, _):
            for u in range(pair):
                part_ = src[c, :, u * rows : (u + 1) * rows]
                if scale is not None:
                    part_ = (part_ * scale).astype(jnp.bfloat16)
                dst[:, columns(c * pair + u)] = part_.T
            return 0

        lax.fori_loop(0, chunks, one, 0)

    def keys(step, _):
        w, half = step // 2, lax.rem(step, 2)
        grads = [dot(kv[w, 1], do_t[c]) for c in chunks_of(half)]
        for c, grad in zip(chunks_of(half), grads):
            ds = (prob_of(w, c) * (grad - delta_s[c])).astype(jnp.bfloat16)
            part[w, 0] += dot_nt(q_t[c], ds)
            dq_t[c] += dot(k_t[w], ds)

        @pl.when(step == 1)
        def _():
            pass_back(0, 0)
            pass_back(2, 1)

        @pl.when(step == 5)
        def _():
            pass_back(1, 0)

        return 0

    lax.fori_loop(0, 2 * WIN, keys, 0)
    unturn(attn_t, attn_ref, None)
    pass_back(2, 0)
    unturn(dq_t, dq_ref, SCALE)
    pass_back(SPAN, 1)
    pass_back(SPAN, 0)

    for group in sends + [kind for hop in halos + backs for kind in hop]:
        for copy in group:
            copy.wait_send()


def settle(*refs):
    n = len(refs) // 2
    copies = [
        pltpu.make_async_copy(refs[i], refs[n + i], refs[-1].at[i]) for i in range(n)
    ]
    for copy in copies:
        copy.start()
    for copy in copies:
        copy.wait()


def per_device(n_seq, n_kvh, query_in, key_in, value_in, grad_out, doc_lengths):
    rows, cols = grad_out.shape
    chunks, wide = cols // (D * PAIR), PAIR * rows
    bf16, f32 = jnp.bfloat16, jnp.float32
    vmem = pl.BlockSpec(memory_space=pltpu.VMEM)
    hbm = pl.BlockSpec(memory_space=pltpu.HBM)
    dma = pltpu.SemaphoreType.DMA
    shapes = (
        jax.ShapeDtypeStruct((rows, cols), bf16),
        jax.ShapeDtypeStruct((rows, cols), bf16),
        jax.ShapeDtypeStruct((rows, D), bf16),
        jax.ShapeDtypeStruct((rows, D), bf16),
    )
    results = pl.pallas_call(
        functools.partial(kernel, n_seq, n_kvh),
        out_shape=tuple(pltpu.VMEM(shape.shape, shape.dtype) for shape in shapes),
        in_specs=[vmem, hbm, hbm, hbm, hbm],
        out_specs=(vmem, vmem, vmem, vmem),
        scratch_shapes=[
            pltpu.VMEM((rows, cols), bf16),
            pltpu.VMEM((rows, cols), bf16),
            pltpu.VMEM((chunks, D, wide), bf16),
            pltpu.VMEM((chunks, D, wide), bf16),
            pltpu.VMEM((WIN, 2, rows, D), bf16),
            pltpu.VMEM((WIN, D, rows), bf16),
            pltpu.VMEM((WIN, D, rows), bf16),
            pltpu.VMEM((WIN, rows, rows), f32),
            pltpu.VMEM((WIN, chunks, rows, wide), f32),
            pltpu.VMEM((WIN + 1, chunks, 1, wide), f32),
            pltpu.VMEM((WIN, chunks, 1, wide), f32),
            pltpu.VMEM((chunks, D, wide), f32),
            pltpu.VMEM((chunks, D, wide), bf16),
            pltpu.VMEM((chunks, D, wide), f32),
            pltpu.VMEM((WIN, chunks, 1, wide), f32),
            pltpu.VMEM((chunks, 1, wide), f32),
            pltpu.VMEM((WIN, 2, D, rows), f32),
            pltpu.VMEM((SPAN, 2, 2, D, rows // 2), bf16),
            pltpu.VMEM((SPAN, 2, 2, D, rows // 2), bf16),
            dma((4,)),
            dma((4, n_kvh - 1)),
            dma((4, n_kvh - 1)),
            dma((SPAN, 2, 2)),
            dma((SPAN, 2, 2)),
            dma((SPAN, 2, 2)),
            dma((SPAN, 2, 2)),
        ],
        compiler_params=pltpu.CompilerParams(
            collective_id=0, has_side_effects=True, vmem_limit_bytes=48 * 1024 * 1024
        ),
    )(
        *(
            pltpu.with_memory_space_constraint(operand, pltpu.HBM)
            for operand in (doc_lengths.reshape(1, -1), query_in, key_in, value_in, grad_out)
        )
    )
    return pl.pallas_call(
        settle,
        out_shape=shapes,
        in_specs=[vmem] * len(shapes),
        out_specs=(hbm,) * len(shapes),
        scratch_shapes=[dma((len(shapes),))],
    )(*(pltpu.with_memory_space_constraint(result, pltpu.VMEM) for result in results))


def solution(mesh):
    placed = (
        P(("seq", "kvh"), None),
        P(("seq", "kvh"), None),
        P(("seq", "kvh"), None),
        P("seq", "kvh"),
        P(),
    )
    return jax.shard_map(
        functools.partial(per_device, mesh.shape["seq"], mesh.shape["kvh"]),
        mesh=mesh,
        in_specs=placed,
        out_specs=(P("seq", "kvh"), P("seq", "kvh"), P("seq", "kvh"), P("seq", "kvh")),
        check_vma=False,
    )
```

time: 46.2 us -> 49 us (1.061)
  the two profiles are of different devices: /device:TPU:8 before, /device:TPU:32 now
where the time goes in v4:
time: 49 us; the launch traced here: 48.8 us
  Pallas kernels  48.2 us (98%)
  between operations  0.64 us (1%)
    pallas_call x1, Pallas kernels, per_device(): pl.pallas_call(functools.partial(kernel, n_seq, n_kvh), out_shape=tuple((...  47.2 us
    pallas_call x1, Pallas kernels, per_device(): pl.pallas_call(settle, out_shape=shapes, in_specs=[vmem] * len(shapes), o...  1.03 us

profile of v4, /device:TPU:32, one launch (start us, length us, event | category | flops | bytes accessed | tf_op | source)
XLA Modules:
  0.0 48.8 jit_solution(13303336192279754053)
XLA Ops:
  0.6 47.2 %shard_map.84 = (bf16[256,1024]{1,0:T(8,128)(2,1)S(1)}, bf16[256,1024]{1,0:T(8,128)(2,1)S(1)}, bf16[256,128]{1,0:T(8,128)(2,1)S(1)}, bf16[256,128]{1,0:T(8,128)(2,1)S(1)}) custom-call(s32[1,64]{1,0:T(1,128)} %bitcast.1, bf16[32,8192]{1,0:T(8,128)(2,1)} %q_hbm.1, bf16[32,1024]{1,0:T(8,128)(2,1)} %k_hbm.1, bf16[32,1024]{1,0:T(8,128)(2,1)} %v_hbm.1, ...), custom_call_target="tpu_custom_call" | custom-call | tf_op jit(solution)/shard_map/pallas_call | solution.py:416
  47.8 1.0 %shard_map.85 = (bf16[256,1024]{1,0:T(8,128)(2,1)}, bf16[256,1024]{1,0:T(8,128)(2,1)}, bf16[256,128]{1,0:T(8,128)(2,1)}, bf16[256,128]{1,0:T(8,128)(2,1)}) custom-call(bf16[256,1024]{1,0:T(8,128)(2,1)S(1)} %get-tuple-element.8.refs_0_, bf16[256,1024]{1,0:T(8,128)(2,1)S(1)} %get-tuple-element.9.refs_1_, bf16[256,128]{1,0:T(8,128)(2,1)S(1)} %get-tuple-element.10.refs_2_, ...), custom_call_target="tpu_custom_call" | custom-call | tf_op jit(solution)/shard_map/pallas_call | solution.py:458

commit v5 on v3

--- a/solution.py
+++ b/solution.py
@@ -108,17 +108,31 @@
         return pltpu.make_async_remote_copy(
             src_ref=src,
             dst_ref=dst,
-            send_sem=a2a_send.at[kind, j - 1],
-            recv_sem=a2a_recv.at[kind, j - 1],
+            send_sem=a2a_send.at[kind],
+            recv_sem=a2a_recv.at[kind],
             device_id=(s, peer),
             device_id_type=MESH,
         )
 
-    sends = [[to_peer(kind, j) for j in range(1, n_kvh)] for kind in range(4)]
-
-    def start(copies):
-        for copy in copies:
-            copy.start()
+    def send(kind):
+        for j in range(1, n_kvh):
+            to_peer(kind, j).start()
+
+    def all_pieces(kind):
+        size = (n_kvh - 1) * piece
+        half = cols // 2
+        if kind >= 2:
+            place = q_loc.at[:size, pl.ds((kind - 2) * half, half)]
+        else:
+            place = kv.at[SPAN, kind, :size, :]
+        return pltpu.make_async_remote_copy(
+            src_ref=place,
+            dst_ref=place,
+            send_sem=a2a_send.at[kind],
+            recv_sem=a2a_recv.at[kind],
+            device_id=(s, lax.rem(g + 1, n_kvh)),
+            device_id_type=MESH,
+        )
 
     def halo(hop, kind):
         return pltpu.make_async_remote_copy(
@@ -157,12 +171,11 @@
         halos[hop][kind].start()
 
     def take_queries(half):
-        for copy in sends[2 + half]:
-            copy.wait_recv()
+        all_pieces(2 + half).wait_recv()
         for c in range(half * per_half, (half + 1) * per_half):
             turn(q_loc, q_t, c)
 
-    def set_all():
+    def set_mask():
         docs = doc_ref.shape[1]
         lens = jnp.broadcast_to(doc_ref[...].astype(jnp.float32), (docs, docs))
         upto = lax.broadcasted_iota(jnp.int32, (docs, docs), 1) <= lax.broadcasted_iota(
@@ -192,42 +205,24 @@
 
         lax.fori_loop(0, chunks, clear, 0)
 
+    def set_grad():
         locals_[2].wait()
 
-        def set_grad(c, _):
+        def one(c, _):
             turn(do_loc, do_t, c)
             return 0
 
-        lax.fori_loop(0, chunks, set_grad, 0)
-
-    def piece_on(kind, j):
-        place = (
-            pl.ds(pl.multiple_of(lax.rem(g + n_kvh - j, n_kvh) * piece, piece), piece),
-            slice(None),
-        )
-        pltpu.make_async_remote_copy(
-            src_ref=kv.at[(SPAN, kind) + place],
-            dst_ref=kv.at[(SPAN - 1, kind) + place],
-            send_sem=halo_send.at[0, kind],
-            recv_sem=halo_recv.at[0, kind],
-            device_id=(nxt, g),
-            device_id_type=MESH,
-        ).start()
-
-    near_first = sorted(range(1, n_kvh), key=lambda j: min(j, n_kvh - j))
-    for kind in range(2):
-        start(sends[kind])
+        lax.fori_loop(0, chunks, one, 0)
+
+    for kind in range(3):
+        send(kind)
+    set_mask()
     for kind in range(2):
         locals_[kind].wait()
-        piece_on(kind, 0)
-    for kind in range(2, 4):
-        start(sends[kind])
-    for kind in range(2):
-        for j in near_first:
-            sends[kind][j - 1].wait_recv()
-            piece_on(kind, j)
-
-    set_all()
+        all_pieces(kind).wait_recv()
+        halos[0][kind].start()
+    send(3)
+    set_grad()
     turn_kv(SPAN)
     pass_on(1, 0)
     pass_on(1, 1)
@@ -377,7 +372,9 @@
     unturn(dq_t, dq_ref, SCALE)
     pass_back(SPAN)
 
-    for group in sends + halos + backs:
+    for kind in range(4):
+        all_pieces(kind).wait_send()
+    for group in halos + backs:
         for copy in group:
             copy.wait_send()
 
@@ -431,8 +428,8 @@
             pltpu.VMEM((SPAN, 2, D, rows), bf16),
             pltpu.VMEM((SPAN, 2, D, rows), bf16),
             dma((4,)),
-            dma((4, n_kvh - 1)),
-            dma((4, n_kvh - 1)),
+            dma((4,)),
+            dma((4,)),
             dma((SPAN, 2)),
             dma((SPAN, 2)),
             dma((SPAN, 2)),

time: 46.2 us -> 46.9 us (1.015)
  Pallas kernels: 45.5 us -> 46.1 us
    pallas_call x1, Pallas kernels: 44.4 us -> 45.1 us  [per_device(): pl.pallas_call(functools.partial(kernel, n_seq, n_kvh), out_shape=tuple((...]
where the time goes in v5:
time: 46.9 us; the launch traced here: 46.7 us
  Pallas kernels  46.1 us (98%)
  between operations  0.64 us (1%)
    pallas_call x1, Pallas kernels, per_device(): pl.pallas_call(functools.partial(kernel, n_seq, n_kvh), out_shape=tuple((...  45.1 us
    pallas_call x1, Pallas kernels, per_device(): pl.pallas_call(settle, out_shape=shapes, in_specs=[vmem] * len(shapes), o...  1.03 us

profile of v5, /device:TPU:8, one launch (start us, length us, event | category | flops | bytes accessed | tf_op | source)
XLA Modules:
  0.0 46.7 jit_solution(13043667002841296871)
XLA Ops:
  0.6 45.1 %shard_map.84 = (bf16[256,1024]{1,0:T(8,128)(2,1)S(1)}, bf16[256,1024]{1,0:T(8,128)(2,1)S(1)}, bf16[256,128]{1,0:T(8,128)(2,1)S(1)}, bf16[256,128]{1,0:T(8,128)(2,1)S(1)}) custom-call(s32[1,64]{1,0:T(1,128)} %bitcast.1, bf16[32,8192]{1,0:T(8,128)(2,1)} %q_hbm.1, bf16[32,1024]{1,0:T(8,128)(2,1)} %k_hbm.1, bf16[32,1024]{1,0:T(8,128)(2,1)} %v_hbm.1, ...), custom_call_target="tpu_custom_call" | custom-call | tf_op jit(solution)/shard_map/pallas_call | solution.py:406
  45.7 1.0 %shard_map.85 = (bf16[256,1024]{1,0:T(8,128)(2,1)}, bf16[256,1024]{1,0:T(8,128)(2,1)}, bf16[256,128]{1,0:T(8,128)(2,1)}, bf16[256,128]{1,0:T(8,128)(2,1)}) custom-call(bf16[256,1024]{1,0:T(8,128)(2,1)S(1)} %get-tuple-element.8.refs_0_, bf16[256,1024]{1,0:T(8,128)(2,1)S(1)} %get-tuple-element.9.refs_1_, bf16[256,128]{1,0:T(8,128)(2,1)S(1)} %get-tuple-element.10.refs_2_, ...), custom_call_target="tpu_custom_call" | custom-call | tf_op jit(solution)/shard_map/pallas_call | solution.py:447

commit v6 on v5

--- a/solution.py
+++ b/solution.py
@@ -16,7 +16,7 @@
 HIDDEN = -1e30
 SCALE = 1.0 / math.sqrt(D)
 SCALE_2 = SCALE * math.log2(math.e)
-PAIR = 2
+PAIR = 4
 
 
 def dot(a, b):

time: 46.9 us -> 46.4 us (0.989)
  no operation moved by 1% of the time
where the time goes in v6:
time: 46.4 us; the launch traced here: 46.3 us
  Pallas kernels  45.7 us (98%)
  between operations  0.64 us (1%)
    pallas_call x1, Pallas kernels, per_device(): pl.pallas_call(functools.partial(kernel, n_seq, n_kvh), out_shape=tuple((...  44.6 us
    pallas_call x1, Pallas kernels, per_device(): pl.pallas_call(settle, out_shape=shapes, in_specs=[vmem] * len(shapes), o...  1.03 us

profile of v6, /device:TPU:8, one launch (start us, length us, event | category | flops | bytes accessed | tf_op | source)
XLA Modules:
  0.0 46.3 jit_solution(17212756434140286397)
XLA Ops:
  0.6 44.6 %shard_map.84 = (bf16[256,1024]{1,0:T(8,128)(2,1)S(1)}, bf16[256,1024]{1,0:T(8,128)(2,1)S(1)}, bf16[256,128]{1,0:T(8,128)(2,1)S(1)}, bf16[256,128]{1,0:T(8,128)(2,1)S(1)}) custom-call(s32[1,64]{1,0:T(1,128)} %bitcast.1, bf16[32,8192]{1,0:T(8,128)(2,1)} %q_hbm.1, bf16[32,1024]{1,0:T(8,128)(2,1)} %k_hbm.1, bf16[32,1024]{1,0:T(8,128)(2,1)} %v_hbm.1, ...), custom_call_target="tpu_custom_call" | custom-call | tf_op jit(solution)/shard_map/pallas_call | solution.py:406
  45.3 1.0 %shard_map.85 = (bf16[256,1024]{1,0:T(8,128)(2,1)}, bf16[256,1024]{1,0:T(8,128)(2,1)}, bf16[256,128]{1,0:T(8,128)(2,1)}, bf16[256,128]{1,0:T(8,128)(2,1)}) custom-call(bf16[256,1024]{1,0:T(8,128)(2,1)S(1)} %get-tuple-element.8.refs_0_, bf16[256,1024]{1,0:T(8,128)(2,1)S(1)} %get-tuple-element.9.refs_1_, bf16[256,128]{1,0:T(8,128)(2,1)S(1)} %get-tuple-element.10.refs_2_, ...), custom_call_target="tpu_custom_call" | custom-call | tf_op jit(solution)/shard_map/pallas_call | solution.py:447

commit v7 on v3

--- a/solution.py
+++ b/solution.py
@@ -220,12 +220,11 @@
     for kind in range(2):
         locals_[kind].wait()
         piece_on(kind, 0)
-    for kind in range(2, 4):
-        start(sends[kind])
     for kind in range(2):
         for j in near_first:
             sends[kind][j - 1].wait_recv()
             piece_on(kind, j)
+        start(sends[2 + kind])
 
     set_all()
     turn_kv(SPAN)
@@ -280,33 +279,25 @@
 
     def oldest_scores(half, _):
         for c, score in zip(chunks_of(half), scores(0, half)):
-            weigh(0, c, score)
-        return 0
-
-    halos[2][0].wait_recv()
-    lax.fori_loop(0, 2, oldest_scores, 0)
-    halos[2][1].wait_recv()
-    turn_kv(0)
-
-    def oldest_sum(c, _):
-        gather(0, c, prob_s[0, c])
-        return 0
-
-    lax.fori_loop(0, chunks, oldest_sum, 0)
+            prob = weigh(0, c, score)
+            top = max_s[0, c]
+            shares = [jnp.exp2((max_s[w, c] - top) * SCALE_2) for w in range(1, WIN)]
+            before = out_t[c, D : D + 1, :] * shares[0]
+            inv = 1.0 / (before + jnp.sum(prob, axis=0, keepdims=True))
+            ratio_s[0, c] = inv
+            for w in range(1, WIN):
+                ratio_s[w, c] = shares[w - 1] * inv
+        return 0
 
     def finish(c, _):
-        inv = 1.0 / out_t[c, D : D + 1, :]
-        top = max_s[0, c]
-        for w in range(WIN):
-            ratio_s[w, c] = jnp.exp2((max_s[w, c] - top) * SCALE_2) * inv
-        out = (out_t[c, :D, :] * inv).astype(jnp.bfloat16)
+        total = out_t[c, :D, :] * ratio_s[1, c]
+        prob = (prob_s[0, c] * ratio_s[0, c]).astype(jnp.bfloat16)
+        out = (total + dot(v_t[0, :D, :], prob)).astype(jnp.bfloat16)
         attn_t[c] = out
         delta_s[c] = jnp.sum(
             out.astype(jnp.float32) * do_t[c].astype(jnp.float32), axis=0, keepdims=True
         )
         return 0
-
-    lax.fori_loop(0, chunks, finish, 0)
 
     def pass_back(hop, kinds=(1, 0)):
         for kind in kinds:
@@ -350,8 +341,13 @@
             one_dk(0, c, prob_s[0, c] * ratio_s[0, c], grad)
         return 0
 
+    halos[2][0].wait_recv()
+    lax.fori_loop(0, 2, oldest_scores, 0)
     lax.fori_loop(0, 2, oldest_dv, 0)
     pass_back(0, (1,))
+    halos[2][1].wait_recv()
+    turn_kv(0)
+    lax.fori_loop(0, chunks, finish, 0)
     lax.fori_loop(0, 2, oldest_dk, 0)
     pass_back(0, (0,))
 

time: 46.2 us -> 45.8 us (level)
  Pallas kernels: 45.5 us -> 45 us
where the time goes in v7:
time: 45.8 us; the launch traced here: 45.7 us
  Pallas kernels  45 us (98%)
  between operations  0.64 us (1%)
    pallas_call x1, Pallas kernels, per_device(): pl.pallas_call(functools.partial(kernel, n_seq, n_kvh), out_shape=tuple((...  44 us
    pallas_call x1, Pallas kernels, per_device(): pl.pallas_call(settle, out_shape=shapes, in_specs=[vmem] * len(shapes), o...  1.03 us

profile of v7, /device:TPU:8, one launch (start us, length us, event | category | flops | bytes accessed | tf_op | source)
XLA Modules:
  0.0 45.7 jit_solution(14735349276473087575)
XLA Ops:
  0.6 44.0 %shard_map.84 = (bf16[256,1024]{1,0:T(8,128)(2,1)S(1)}, bf16[256,1024]{1,0:T(8,128)(2,1)S(1)}, bf16[256,128]{1,0:T(8,128)(2,1)S(1)}, bf16[256,128]{1,0:T(8,128)(2,1)S(1)}) custom-call(s32[1,64]{1,0:T(1,128)} %bitcast.1, bf16[32,8192]{1,0:T(8,128)(2,1)} %q_hbm.1, bf16[32,1024]{1,0:T(8,128)(2,1)} %k_hbm.1, bf16[32,1024]{1,0:T(8,128)(2,1)} %v_hbm.1, ...), custom_call_target="tpu_custom_call" | custom-call | tf_op jit(solution)/shard_map/pallas_call | solution.py:405
  44.7 1.0 %shard_map.85 = (bf16[256,1024]{1,0:T(8,128)(2,1)}, bf16[256,1024]{1,0:T(8,128)(2,1)}, bf16[256,128]{1,0:T(8,128)(2,1)}, bf16[256,128]{1,0:T(8,128)(2,1)}) custom-call(bf16[256,1024]{1,0:T(8,128)(2,1)S(1)} %get-tuple-element.8.refs_0_, bf16[256,1024]{1,0:T(8,128)(2,1)S(1)} %get-tuple-element.9.refs_1_, bf16[256,128]{1,0:T(8,128)(2,1)S(1)} %get-tuple-element.10.refs_2_, ...), custom_call_target="tpu_custom_call" | custom-call | tf_op jit(solution)/shard_map/pallas_call | solution.py:446
